TPU v7x, 512 devices: a whole 4x4x16 slice. The times are simulated.
512 devices in a mesh: src: 32 (over y_lo, z), tp: 16 (over x, y_hi, core).
Axes of the slice: x: 4, y: 4 (y_hi: 2, y_lo: 2; y = y_hi * 2 + y_lo), z: 16, core: 2. Of those that a mesh axis runs over, the one named last changes fastest.
Arguments:
- stream: float32 [64, 16384], P(None, 'src'), may hold values from -32 to 32
- norm_gain: float32 [16384], P('src'), may hold values from 0.1 to 1.9
- frozen_up_weight: bfloat16 [16384, 28672], P('src', 'tp'), may hold values from -0.046875 to 0.046875
- factor_a: bfloat16 [64, 16384], P('tp', 'src'), may hold values from -0.046875 to 0.046875
- factor_b: bfloat16 [64, 28672], P('src', 'tp'), may hold values from -0.1796875 to 0.1796875
- down_projection_matrix: bfloat16 [28672, 16384], P('tp', 'src'), may hold values from -0.03125 to 0.03125
Outputs:
- final_stream: float32 [64, 16384], P(None, 'src')
All inputs are finite; a program needn't handle non-finite values.
Results may differ from a plain program's by a relative error of at most 0.0037.
Values may be sent and summed in bfloat16 or wider, within the bound.
No kernel may reach another device: no remote copies, remote signals or barrier semaphores. Data moves between devices by JAX's collectives and lax.ppermute only.
A program may use at most 64 MiB of HBM per device.

v0:
```python
import jax
import jax.numpy as jnp
from jax import lax
from jax.sharding import PartitionSpec as P

D = 16384
STEPS = 3


ADAPTER_SCALING = 2.0
EPSILON = 1e-05


def per_device(stream, norm_gain, frozen_up_weight, factor_a, factor_b, down_projection_matrix):
    ranks_a = lax.all_gather(factor_a, "tp", axis=0, tiled=True)
    ranks_b = lax.all_gather(factor_b, "src", axis=0, tiled=True)
    low_rank_update = lax.dot_general(
        ranks_a, ranks_b, (((0,), (0,)), ((), ())), preferred_element_type=jnp.float32
    )
    merged_up_weight = (
        frozen_up_weight.astype(jnp.float32) + ADAPTER_SCALING * low_rank_update
    ).astype(jnp.bfloat16)
    current = stream
    for step in range(STEPS):
        local_squares = jnp.sum(current * current, axis=1)
        scaled = (current * norm_gain).astype(jnp.bfloat16)
        partial_up = jnp.dot(scaled, merged_up_weight, preferred_element_type=jnp.float32)
        combined_output, squares = lax.psum((partial_up, local_squares), "src")
        hidden = combined_output * lax.rsqrt(squares / D + EPSILON)[:, None]
        active = jax.nn.silu(hidden).astype(jnp.bfloat16)
        branch = jnp.dot(active, down_projection_matrix, preferred_element_type=jnp.float32)
        current = current + lax.psum(branch, "tp")
    return current


def solution(mesh):
    in_specs = (
        P(None, "src"),
        P("src"),
        P("src", "tp"),
        P("tp", "src"),
        P("src", "tp"),
        P("tp", "src"),
    )
    out_specs = P(None, "src")
    return jax.shard_map(
        per_device, mesh=mesh, in_specs=in_specs, out_specs=out_specs, check_vma=False
    )
```

profile of v0, /device:TPU:1, one launch (start us, length us, event | category | flops | bytes accessed | tf_op | source)
XLA Modules:
  0.0 1322.7 jit_solution(14942531557362787316)
XLA Ops:
  6.5 0.0 copy-start
  6.5 0.0 all-reduce.7.cloned.1.call-start
  6.5 26.3 %all-gather = bf16[16,4,512]{2,1,0:T(4,128)(2,1)S(1)} all-gather(bf16[1,4,512]{2,1,0:T(4,128)(2,1)} %bitcast.11), channel_id=1, replica_groups=mesh['src'=32,'tp'=16] {'tp'}, dimensions={0}, use_global_device_ids=true | all-gather | bytes 69632 | tf_op jit(solution)/shard_map/all_gather | solution.py:15
  32.8 55.2 %all-gather.1 = bf16[32,2,1792]{2,1,0:T(2,128)(2,1)S(1)} all-gather(bf16[1,2,1792]{2,1,0:T(2,128)(2,1)} %bitcast.10), channel_id=1, replica_groups=mesh['src'=32,'tp'=16] {'src'}, dimensions={0}, use_global_device_ids=true | all-gather | bytes 236544 | tf_op jit(solution)/shard_map/all_gather | solution.py:16
  88.0 0.1 reshape.7
  88.1 0.0 copy-start.2
  88.1 0.0 copy-start.3
  88.2 2.2 add_convert_fusion
  90.4 0.0 copy-start.1
  90.4 1.2 copy-done.1
  91.6 0.0 copy-done.2
  91.6 0.0 copy-done.3
  91.6 1.2 fusion.9
  92.8 0.0 all-reduce.7.cloned.1.call-update
  92.8 0.0 all-reduce.9.cloned.1.call-start
  92.9 0.1 multiply_reduce_fusion.2
  93.0 47.3 %psum.64 = f32[64]{0:T(128)S(1)} all-reduce(f32[64]{0:T(128)S(1)} %multiply_reduce_fusion.2), channel_id=1, replica_groups=mesh['src'=32,'tp'=16] {'src'}, use_global_device_ids=true, to_apply=%region_2.0 | all-reduce | flops 64 | bytes 512 | tf_op jit(solution)/shard_map/psum | solution.py:28
  140.3 186.9 %all-reduce.7.cloned.1.call-done = f32[64,1792]{1,0:T(8,128)} async-done(((f32[64,1792]{1,0:T(8,128)}), f32[64,1792]{1,0:T(8,128)}) %all-reduce.7.cloned.1.call-update) | async-done | bytes 458768 | tf_op jit(solution)/shard_map/psum | solution.py:28
  327.3 0.0 copy-done
  327.3 2.2 fusion
  329.5 0.0 all-reduce.9.cloned.1.call-update
  329.5 0.0 all-reduce.11.cloned.1.call-start
  329.5 167.6 %all-reduce.9.cloned.1.call-done = f32[64,512]{1,0:T(8,128)} async-done(((f32[64,512]{1,0:T(8,128)}), f32[64,512]{1,0:T(8,128)}) %all-reduce.9.cloned.1.call-update) | async-done | bytes 131088 | tf_op jit(solution)/shard_map/psum | solution.py:32
  497.1 1.0 multiply_reduce_fusion.1
  498.2 2.7 fusion.10
  500.9 0.0 all-reduce.11.cloned.1.call-update
  500.9 0.0 all-reduce.13.cloned.1.call-start
  500.9 51.2 %psum.67 = f32[64]{0:T(128)S(1)} all-reduce(f32[64]{0:T(128)S(1)} %get-tuple-element.7), channel_id=1, replica_groups=mesh['src'=32,'tp'=16] {'src'}, use_global_device_ids=true, to_apply=%region_6.7 | all-reduce | flops 64 | bytes 512 | tf_op jit(solution)/shard_map/psum | solution.py:28
  552.1 183.9 %all-reduce.11.cloned.1.call-done = f32[64,1792]{1,0:T(8,128)} async-done(((f32[64,1792]{1,0:T(8,128)}), f32[64,1792]{1,0:T(8,128)}) %all-reduce.11.cloned.1.call-update) | async-done | bytes 458768 | tf_op jit(solution)/shard_map/psum | solution.py:28
  736.0 2.2 fusion.1
  738.2 0.0 all-reduce.13.cloned.1.call-update
  738.2 0.0 all-reduce.15.cloned.1.call-start
  738.2 167.5 %all-reduce.13.cloned.1.call-done = f32[64,512]{1,0:T(8,128)} async-done(((f32[64,512]{1,0:T(8,128)}), f32[64,512]{1,0:T(8,128)}) %all-reduce.13.cloned.1.call-update) | async-done | bytes 131088 | tf_op jit(solution)/shard_map/psum | solution.py:32
  905.7 1.0 multiply_reduce_fusion
  906.7 2.7 fusion.11
  909.4 0.0 all-reduce.15.cloned.1.call-update
  909.5 0.0 all-reduce.17.cloned.1.call-start
  909.5 51.2 %psum.70 = f32[64]{0:T(128)S(1)} all-reduce(f32[64]{0:T(128)S(1)} %get-tuple-element.5), channel_id=1, replica_groups=mesh['src'=32,'tp'=16] {'src'}, use_global_device_ids=true, to_apply=%region_10.11 | all-reduce | flops 64 | bytes 512 | tf_op jit(solution)/shard_map/psum | solution.py:28
  960.7 183.9 %all-reduce.15.cloned.1.call-done = f32[64,1792]{1,0:T(8,128)} async-done(((f32[64,1792]{1,0:T(8,128)}), f32[64,1792]{1,0:T(8,128)}) %all-reduce.15.cloned.1.call-update) | async-done | bytes 458768 | tf_op jit(solution)/shard_map/psum | solution.py:28
  1144.6 2.2 fusion.2
  1146.7 0.0 all-reduce.17.cloned.1.call-update
  1146.7 167.5 %all-reduce.17.cloned.1.call-done = f32[64,512]{1,0:T(8,128)} async-done(((f32[64,512]{1,0:T(8,128)}), f32[64,512]{1,0:T(8,128)}) %all-reduce.17.cloned.1.call-update) | async-done | bytes 131088 | tf_op jit(solution)/shard_map/psum | solution.py:32
  1314.3 1.6 add.58
  (4 shorter events, 0.0 us)
Async XLA Ops:
  6.5 320.7 %copy-start = (bf16[1792,512]{1,0:T(8,128)(2,1)S(1)}, bf16[1792,512]{1,0:T(8,128)(2,1)}, u32[]{:S(2)}) copy-start(bf16[1792,512]{1,0:T(8,128)(2,1)} %param.11) | copy-start | bytes 5505028
  6.5 320.7 %all-reduce.7.cloned.1.call-start = ((), (), s32[]{:S(2)}) async-start(), calls=%async_computation | async-start | bytes 917504 | tf_op jit(solution)/shard_map/psum | solution.py:28
  88.1 3.5 copy-start.2
  88.1 3.5 copy-start.3
  90.4 1.3 copy-start.1
  92.8 404.3 %all-reduce.9.cloned.1.call-start = ((), (), s32[]{:S(2)}) async-start(), calls=%async_computation.1 | async-start | bytes 262144 | tf_op jit(solution)/shard_map/psum | solution.py:32
  329.5 406.5 %all-reduce.11.cloned.1.call-start = ((), (), s32[]{:S(2)}) async-start(), calls=%async_computation.2 | async-start | bytes 917504 | tf_op jit(solution)/shard_map/psum | solution.py:28
  500.9 404.8 %all-reduce.13.cloned.1.call-start = ((), (), s32[]{:S(2)}) async-start(), calls=%async_computation.3 | async-start | bytes 262144 | tf_op jit(solution)/shard_map/psum | solution.py:32
  738.2 406.4 %all-reduce.15.cloned.1.call-start = ((), (), s32[]{:S(2)}) async-start(), calls=%async_computation.4 | async-start | bytes 917504 | tf_op jit(solution)/shard_map/psum | solution.py:28
  909.5 404.8 %all-reduce.17.cloned.1.call-start = ((), (), s32[]{:S(2)}) async-start(), calls=%async_computation.5 | async-start | bytes 262144 | tf_op jit(solution)/shard_map/psum | solution.py:32
Sparse Core Ops, SparseCore 0:
  93.0 234.2 all-reduce.6
  330.4 166.6 all-reduce.8
  501.0 234.9 all-reduce.10
  739.0 166.6 all-reduce.12
  909.6 234.9 all-reduce.14
  1147.6 166.6 all-reduce.16
where the time goes:
time: 1320 us
  waiting for transfers between devices  1060 us (80%)
  blocking collectives  231 us (18%)
  matrix products  15.3 us (1%)
  between operations  13.5 us (1%)
    psum x3, waiting for transfers between devices, per_device(): combined_output, squares = lax.psum((partial_up, local_squares), 'src')  555 us
    psum x3, waiting for transfers between devices, per_device(): current = current + lax.psum(branch, 'tp')  503 us
    psum x3, blocking collectives, per_device(): combined_output, squares = lax.psum((partial_up, local_squares), 'src')  150 us
    all_gather x1, blocking collectives, per_device(): ranks_b = lax.all_gather(factor_b, 'src', axis=0, tiled=True)  55.2 us
  transfers between devices with their start and end apart: 6, of which 6 were waited for; matrix products, arithmetic and copies ran while one was open for 0% of the time, Pallas kernels for 0%

commit v1 on v0

v1 whole, which is shorter than its diff:
```python
import jax
import jax.numpy as jnp
from jax import lax
from jax.sharding import PartitionSpec as P

D = 16384
STEPS = 3
LANES = 128

ADAPTER_SCALING = 2.0
EPSILON = 1e-05

NEAR = [[y * 16 + far * 4 + low for y in range(2) for low in range(4)] for far in range(4)]
FAR = [[y * 16 + far * 4 + low for far in range(4)] for y in range(2) for low in range(4)]
CORES = [[2 * chip, 2 * chip + 1] for chip in range(8)]
CHIPS = [[2 * chip + core for chip in range(8)] for core in range(2)]


def exchange(blocks, axis, groups):
    return lax.all_to_all(blocks, axis, 0, 0, axis_index_groups=groups, tiled=True)


def share(block, axis, groups, size):
    return exchange(jnp.broadcast_to(block[None], (size,) + block.shape), axis, groups)


def total(blocks):
    return jnp.sum(blocks.astype(jnp.float32), axis=0)


def with_squares(values, squares):
    high = lax.reduce_precision(squares, 8, 7)
    rest = squares - high
    middle = lax.reduce_precision(rest, 8, 7)
    low = rest - middle
    parts = jnp.concatenate(
        [high, middle, low, jnp.zeros((values.shape[0], LANES - 3), jnp.float32)], axis=1
    )
    return jnp.concatenate([values, parts], axis=1).astype(jnp.bfloat16)


def split_squares(both):
    values, parts = both[:, :-LANES], both[:, -LANES:]
    return values, jnp.sum(parts[:, :3], axis=1, keepdims=True)


def per_device(stream, norm_gain, frozen_up_weight, factor_a, factor_b, down_projection_matrix):
    rows, width = stream.shape
    hidden_units = frozen_up_weight.shape[1]
    ranks_a = share(factor_a, "tp", None, 16).reshape(-1, width)
    ranks_b = share(factor_b, "src", None, 32).reshape(-1, hidden_units)
    low_rank_update = lax.dot_general(
        ranks_a, ranks_b, (((0,), (0,)), ((), ())), preferred_element_type=jnp.float32
    )
    merged_up_weight = (
        frozen_up_weight.astype(jnp.float32) + ADAPTER_SCALING * low_rank_update
    ).astype(jnp.bfloat16)
    current = stream
    for step in range(STEPS):
        local_squares = jnp.sum(current * current, axis=1, keepdims=True)
        scaled = (current * norm_gain).astype(jnp.bfloat16)
        partial_up = jnp.dot(scaled, merged_up_weight, preferred_element_type=jnp.float32)
        sent = with_squares(partial_up, local_squares)
        near = total(exchange(sent.reshape(8, rows // 8, -1), "src", NEAR))
        near_values, near_squares = split_squares(near)
        far = total(share(with_squares(near_values, near_squares), "src", FAR, 4))
        combined_output, squares = split_squares(far)
        hidden = combined_output * lax.rsqrt(squares / D + EPSILON)
        active = jax.nn.silu(hidden).astype(jnp.bfloat16)
        active = share(active, "src", NEAR, 8).reshape(rows, hidden_units)
        branch = jnp.dot(active, down_projection_matrix, preferred_element_type=jnp.float32)
        branch = total(share(branch.astype(jnp.bfloat16), "tp", CORES, 2))
        branch = total(share(branch.astype(jnp.bfloat16), "tp", CHIPS, 8))
        current = current + branch
    return current


def solution(mesh):
    in_specs = (
        P(None, "src"),
        P("src"),
        P("src", "tp"),
        P("tp", "src"),
        P("src", "tp"),
        P("tp", "src"),
    )
    out_specs = P(None, "src")
    return jax.shard_map(
        per_device, mesh=mesh, in_specs=in_specs, out_specs=out_specs, check_vma=False
    )
```

time: 1320 us -> 241 us (0.18)
  waiting for transfers between devices: 1060 us -> 17.5 us
  blocking collectives: 231 us -> 191 us
  starting transfers between devices: 0.21 us -> 14.2 us
    psum x6 -> x0, waiting for transfers between devices: 1060 us -> none  [the longest x3 555 us: per_device(): combined_output, squares = lax.psum((partial_up, local_squares), 'src')]
    all_to_all x0 -> x16, blocking collectives: none -> 191 us  [exchange(): lax.all_to_all(blocks, axis, 0, 0, axis_index_groups=groups, tiled=True)]
    psum x3 -> x0, blocking collectives: 150 us -> none  [per_device(): combined_output, squares = lax.psum((partial_up, local_squares), 'src')]
    all_gather x2 -> x0, blocking collectives: 81.5 us -> none  [the longest x1 55.2 us: per_device(): ranks_b = lax.all_gather(factor_b, 'src', axis=0, tiled=True)]
    all_to_all x0 -> x1, waiting for transfers between devices: none -> 17.5 us  [exchange(): lax.all_to_all(blocks, axis, 0, 0, axis_index_groups=groups, tiled=True)]
    all_to_all x0 -> x1, starting transfers between devices: none -> 14.2 us  [exchange(): lax.all_to_all(blocks, axis, 0, 0, axis_index_groups=groups, tiled=True)]
  transfers between devices with their start and end apart: 6 -> 1, of which waited for: 6 -> 1; matrix products, arithmetic and copies ran while one was open for 0% -> 1% of each run, Pallas kernels for 0% -> 0%
where the time goes in v1:
time: 241 us; the launch traced here: 240 us
  blocking collectives  191 us (79%)
  waiting for transfers between devices  17.5 us (7%)
  starting transfers between devices  14.2 us (6%)
  local copies, waits for them, and re-layouts  6.9 us (3%)
  matrix products  6.3 us (3%)
  other arithmetic  3.45 us (1%)
    all_to_all x16, blocking collectives, exchange(): lax.all_to_all(blocks, axis, 0, 0, axis_index_groups=groups, tiled=True)  191 us
    all_to_all x1, waiting for transfers between devices, exchange(): lax.all_to_all(blocks, axis, 0, 0, axis_index_groups=groups, tiled=True)  17.5 us
    all_to_all x1, starting transfers between devices, exchange(): lax.all_to_all(blocks, axis, 0, 0, axis_index_groups=groups, tiled=True)  14.2 us
  transfers between devices with their start and end apart: 1, of which 1 were waited for; matrix products, arithmetic and copies ran while one was open for 1% of the time, Pallas kernels for 0%

profile of v1, /device:TPU:1, one launch (start us, length us, event | category | flops | bytes accessed | tf_op | source)
XLA Modules:
  0.0 239.6 jit_solution(11300355461946460659)
XLA Ops:
  0.0 0.8 broadcast_in_dim.28
  0.8 16.7 %all_to_all.85 = bf16[16,4,512]{2,1,0:T(4,128)(2,1)S(1)} all-to-all(bf16[16,4,512]{2,1,0:T(4,128)(2,1)S(1)} %broadcast_in_dim.28), channel_id=1, replica_groups=mesh['src'=32,'tp'=16] {'tp'}, dimensions={0} | all-to-all | bytes 131072 | tf_op jit(solution)/shard_map/all_to_all | solution.py:20
  17.6 1.5 broadcast_in_dim.29
  19.0 14.2 %all-to-all-start.1 = ((bf16[32,2,1792]{2,1,0:T(2,128)(2,1)}), bf16[32,2,1792]{2,1,0:T(2,128)(2,1)S(1)}, u32[]{:S(2)}, u32[]{:S(2)}) async-start(bf16[32,2,1792]{2,1,0:T(2,128)(2,1)} %broadcast_in_dim.29), calls=%async_computation.1 | async-start | bytes 458752 | tf_op jit(solution)/shard_map/all_to_all | solution.py:20
  33.3 1.0 multiply_reduce_fusion.2
  34.4 0.1 copy.42
  34.5 0.1 copy.41
  34.7 0.1 copy.40
  34.8 17.5 %all-to-all-done.1 = bf16[32,2,1792]{2,1,0:T(2,128)(2,1)S(1)} async-done(((bf16[32,2,1792]{2,1,0:T(2,128)(2,1)}), bf16[32,2,1792]{2,1,0:T(2,128)(2,1)S(1)}, u32[]{:S(2)}, u32[]{:S(2)}) %all-to-all-start.1) | async-done | bytes 229408 | tf_op jit(solution)/shard_map/all_to_all | solution.py:20
  52.4 2.2 add_convert_fusion
  54.7 1.2 copy-done.1
  55.9 0.4 fusion
  56.5 10.5 %all_to_all.86 = bf16[8,8,1920]{2,1,0:T(8,128)(2,1)S(1)} all-to-all(bf16[8,8,1920]{2,1,0:T(8,128)(2,1)S(1)} %concatenate.51), channel_id=1, replica_groups={{0,16,32,48,256,272,288,304},{64,80,96,112,320,336,352,368},{128,144,16..., dimensions={0} | all-to-all | bytes 491520 | tf_op jit(solution)/shard_map/all_to_all | solution.py:20
  67.0 0.1 slice_reduce_fusion.5
  67.5 15.9 %all_to_all.87 = bf16[4,8,1920]{2,1,0:T(8,128)(2,1)S(1)} all-to-all(bf16[4,8,1920]{2,1,0:T(8,128)(2,1)S(1)} %broadcast_in_dim.30), channel_id=1, replica_groups={{0,64,128,192},{16,80,144,208},{32,96,160,224},{48,112,176,240},{256,32..., dimensions={0} | all-to-all | bytes 245760 | tf_op jit(solution)/shard_map/all_to_all | solution.py:20
  83.5 0.1 slice_reduce_fusion.4
  83.8 9.6 %all_to_all.88 = bf16[8,8,1792]{2,1,0:T(8,128)(2,1)S(1)} all-to-all(bf16[8,8,1792]{2,1,0:T(8,128)(2,1)S(1)} %broadcast_in_dim.31), channel_id=1, replica_groups={{0,16,32,48,256,272,288,304},{64,80,96,112,320,336,352,368},{128,144,16..., dimensions={0} | all-to-all | bytes 458752 | tf_op jit(solution)/shard_map/all_to_all | solution.py:20
  93.3 0.4 convolution_convert_fusion.5
  93.8 9.7 %all_to_all.89 = bf16[2,64,512]{2,1,0:T(8,128)(2,1)S(1)} all-to-all(bf16[2,64,512]{2,1,0:T(8,128)(2,1)S(1)} %broadcast_in_dim.32), channel_id=1, replica_groups={{0,1},{2,3},{4,5},{6,7},{8,9},{10,11},{12,13},{14,15},{16,17},{18,19},{..., dimensions={0} | all-to-all | bytes 262144 | tf_op jit(solution)/shard_map/all_to_all | solution.py:20
  103.6 12.7 %all_to_all.90 = bf16[8,64,512]{2,1,0:T(8,128)(2,1)S(1)} all-to-all(bf16[8,64,512]{2,1,0:T(8,128)(2,1)S(1)} %broadcast_in_dim.33), channel_id=1, replica_groups={{0,2,4,6,8,10,12,14},{1,3,5,7,9,11,13,15},{16,18,20,22,24,26,28,30},{17..., dimensions={0} | all-to-all | bytes 1048576 | tf_op jit(solution)/shard_map/all_to_all | solution.py:20
  116.3 0.1 multiply_reduce_fusion.1
  116.5 0.1 copy.50
  116.7 0.1 copy.49
  116.8 0.1 copy.48
  116.9 2.0 fusion.1
  119.0 9.8 %all_to_all.91 = bf16[8,8,1920]{2,1,0:T(8,128)(2,1)S(1)} all-to-all(bf16[8,8,1920]{2,1,0:T(8,128)(2,1)S(1)} %concatenate.55), channel_id=1, replica_groups={{0,16,32,48,256,272,288,304},{64,80,96,112,320,336,352,368},{128,144,16..., dimensions={0} | all-to-all | bytes 491520 | tf_op jit(solution)/shard_map/all_to_all | solution.py:20
  128.8 0.1 slice_reduce_fusion.3
  129.4 14.4 %all_to_all.92 = bf16[4,8,1920]{2,1,0:T(8,128)(2,1)S(1)} all-to-all(bf16[4,8,1920]{2,1,0:T(8,128)(2,1)S(1)} %broadcast_in_dim.34), channel_id=1, replica_groups={{0,64,128,192},{16,80,144,208},{32,96,160,224},{48,112,176,240},{256,32..., dimensions={0} | all-to-all | bytes 245760 | tf_op jit(solution)/shard_map/all_to_all | solution.py:20
  143.8 0.1 slice_reduce_fusion.2
  144.1 9.6 %all_to_all.93 = bf16[8,8,1792]{2,1,0:T(8,128)(2,1)S(1)} all-to-all(bf16[8,8,1792]{2,1,0:T(8,128)(2,1)S(1)} %broadcast_in_dim.35), channel_id=1, replica_groups={{0,16,32,48,256,272,288,304},{64,80,96,112,320,336,352,368},{128,144,16..., dimensions={0} | all-to-all | bytes 458752 | tf_op jit(solution)/shard_map/all_to_all | solution.py:20
  153.6 0.4 convolution_convert_fusion.4
  154.1 9.6 %all_to_all.94 = bf16[2,64,512]{2,1,0:T(8,128)(2,1)S(1)} all-to-all(bf16[2,64,512]{2,1,0:T(8,128)(2,1)S(1)} %broadcast_in_dim.36), channel_id=1, replica_groups={{0,1},{2,3},{4,5},{6,7},{8,9},{10,11},{12,13},{14,15},{16,17},{18,19},{..., dimensions={0} | all-to-all | bytes 262144 | tf_op jit(solution)/shard_map/all_to_all | solution.py:20
  163.8 14.1 %all_to_all.95 = bf16[8,64,512]{2,1,0:T(8,128)(2,1)S(1)} all-to-all(bf16[8,64,512]{2,1,0:T(8,128)(2,1)S(1)} %broadcast_in_dim.37), channel_id=1, replica_groups={{0,2,4,6,8,10,12,14},{1,3,5,7,9,11,13,15},{16,18,20,22,24,26,28,30},{17..., dimensions={0} | all-to-all | bytes 1048576 | tf_op jit(solution)/shard_map/all_to_all | solution.py:20
  178.0 0.1 multiply_reduce_fusion
  178.1 0.4 fusion.2
  178.6 0.1 copy.58
  178.8 0.1 copy.57
  178.9 0.1 copy.56
  179.1 0.1 concatenate.58
  179.2 9.8 %all_to_all.96 = bf16[8,8,1920]{2,1,0:T(8,128)(2,1)S(1)} all-to-all(bf16[8,8,1920]{2,1,0:T(8,128)(2,1)S(1)} %concatenate.58), channel_id=1, replica_groups={{0,16,32,48,256,272,288,304},{64,80,96,112,320,336,352,368},{128,144,16..., dimensions={0} | all-to-all | bytes 491520 | tf_op jit(solution)/shard_map/all_to_all | solution.py:20
  189.0 0.1 slice_reduce_fusion.1
  189.6 15.1 %all_to_all.97 = bf16[4,8,1920]{2,1,0:T(8,128)(2,1)S(1)} all-to-all(bf16[4,8,1920]{2,1,0:T(8,128)(2,1)S(1)} %broadcast_in_dim.38), channel_id=1, replica_groups={{0,64,128,192},{16,80,144,208},{32,96,160,224},{48,112,176,240},{256,32..., dimensions={0} | all-to-all | bytes 245760 | tf_op jit(solution)/shard_map/all_to_all | solution.py:20
  204.7 0.1 slice_reduce_fusion
  204.9 9.6 %all_to_all.98 = bf16[8,8,1792]{2,1,0:T(8,128)(2,1)S(1)} all-to-all(bf16[8,8,1792]{2,1,0:T(8,128)(2,1)S(1)} %broadcast_in_dim.39), channel_id=1, replica_groups={{0,16,32,48,256,272,288,304},{64,80,96,112,320,336,352,368},{128,144,16..., dimensions={0} | all-to-all | bytes 458752 | tf_op jit(solution)/shard_map/all_to_all | solution.py:20
  214.5 0.4 convolution_convert_fusion.3
  215.0 9.8 %all_to_all.99 = bf16[2,64,512]{2,1,0:T(8,128)(2,1)S(1)} all-to-all(bf16[2,64,512]{2,1,0:T(8,128)(2,1)S(1)} %broadcast_in_dim.40), channel_id=1, replica_groups={{0,1},{2,3},{4,5},{6,7},{8,9},{10,11},{12,13},{14,15},{16,17},{18,19},{..., dimensions={0} | all-to-all | bytes 262144 | tf_op jit(solution)/shard_map/all_to_all | solution.py:20
  224.9 14.0 %all_to_all.100 = bf16[8,64,512]{2,1,0:T(8,128)(2,1)S(1)} all-to-all(bf16[8,64,512]{2,1,0:T(8,128)(2,1)S(1)} %broadcast_in_dim.41), channel_id=1, replica_groups={{0,2,4,6,8,10,12,14},{1,3,5,7,9,11,13,15},{16,18,20,22,24,26,28,30},{17..., dimensions={0} | all-to-all | bytes 1048576 | tf_op jit(solution)/shard_map/all_to_all | solution.py:20
  239.0 0.7 add.55
  (69 shorter events, 2.8 us)
Async XLA Ops:
  0.0 93.3 %copy-start = (bf16[1792,512]{1,0:T(8,128)(2,1)S(1)}, bf16[1792,512]{1,0:T(8,128)(2,1)}, u32[]{:S(2)}) copy-start(bf16[1792,512]{1,0:T(8,128)(2,1)} %param.11) | copy-start | bytes 5505028
  19.0 33.3 %all-to-all-start.1 = ((bf16[32,2,1792]{2,1,0:T(2,128)(2,1)}), bf16[32,2,1792]{2,1,0:T(2,128)(2,1)S(1)}, u32[]{:S(2)}, u32[]{:S(2)}) async-start(bf16[32,2,1792]{2,1,0:T(2,128)(2,1)} %broadcast_in_dim.29), calls=%async_computation.1 | async-start | bytes 458752 | tf_op jit(solution)/shard_map/all_to_all | solution.py:20
  52.4 3.5 %copy-start.3 = (f32[64,512]{1,0:T(8,128)S(1)}, f32[64,512]{1,0:T(8,128)}, u32[]{:S(2)}) copy-start(f32[64,512]{1,0:T(8,128)} %param.6) | copy-start | bytes 393220
  52.4 3.5 %copy-start.4 = (f32[512]{0:T(512)S(1)}, f32[512]{0:T(512)}, u32[]{:S(2)}) copy-start(f32[512]{0:T(512)} %param.7) | copy-start | bytes 6148
  54.6 1.3 copy-start.1
  163.7 14.4 %copy-start.2 = (bf16[512,1792]{1,0:T(8,128)(2,1)S(1)}, bf16[512,1792]{1,0:T(8,128)(2,1)}, u32[]{:S(2)}) copy-start(bf16[512,1792]{1,0:T(8,128)(2,1)} %copy-done.1) | copy-start | bytes 5505028

commit v2 on v0

v2 whole, which is shorter than its diff:
```python
import jax
import jax.numpy as jnp
from jax import lax
from jax.sharding import PartitionSpec as P

D = 16384
STEPS = 3
LANES = 128

ADAPTER_SCALING = 2.0
EPSILON = 1e-05

NEAR = [[y * 16 + far * 4 + low for y in range(2) for low in range(4)] for far in range(4)]
FAR = [[y * 16 + far * 4 + low for far in range(4)] for y in range(2) for low in range(4)]
PAIRS = [
    [src * 16 + chip * 2 + core for core in range(2) for src in near]
    for near in NEAR
    for chip in range(8)
]
CORES = [[2 * chip, 2 * chip + 1] for chip in range(8)]
CHIPS = [[2 * chip + core for chip in range(8)] for core in range(2)]
SWAP = [(i, i ^ 1) for i in range(16)]


def exchange(blocks, axis, groups):
    return lax.all_to_all(blocks, axis, 0, 0, axis_index_groups=groups, tiled=True)


def share(block, axis, groups, size):
    return exchange(jnp.broadcast_to(block[None], (size,) + block.shape), axis, groups)


def total(blocks):
    return jnp.sum(blocks.astype(jnp.float32), axis=0)


def pack(values, squares, others=None):
    high = lax.reduce_precision(squares, 8, 7)
    rest = squares - high
    middle = lax.reduce_precision(rest, 8, 7)
    parts = [values, high, middle, rest - middle]
    used = 3
    if others is not None:
        parts.append(others)
        used += others.shape[1]
    parts.append(jnp.zeros((values.shape[0], LANES - used), jnp.float32))
    return jnp.concatenate(parts, axis=1).astype(jnp.bfloat16)


def unpack(both, width):
    return both[:, :width], jnp.sum(both[:, width : width + 3], axis=1, keepdims=True)


def activate(values, squares):
    hidden = values * lax.rsqrt(squares / D + EPSILON)
    return jax.nn.silu(hidden).astype(jnp.bfloat16)


def dot(a, b):
    return jnp.dot(a, b, preferred_element_type=jnp.float32)


def per_device(stream, norm_gain, frozen_up_weight, factor_a, factor_b, down_projection_matrix):
    rows, width = stream.shape
    units = frozen_up_weight.shape[1]
    half = rows // 2
    core = lax.axis_index("tp") % 2
    first = core == 0

    down_own = down_projection_matrix
    down_other = lax.ppermute(down_own, "tp", SWAP)

    ranks_a = share(factor_a, "tp", None, 16)
    ranks_a = ranks_a.reshape(2, 4, 4, 2, width).transpose(1, 0, 2, 3, 4).reshape(-1, width)
    ranks = ranks_a.shape[0]

    ordered = stream.reshape(2, 8, rows // 16, width).transpose(1, 0, 2, 3).reshape(rows, width)
    scaled = (ordered * norm_gain).astype(jnp.bfloat16)
    squares = jnp.sum(ordered * ordered, axis=1, keepdims=True)
    projected = lax.dot_general(
        scaled, ranks_a, (((1,), (1,)), ((), ())), preferred_element_type=jnp.float32
    )
    sent = pack(dot(scaled, frozen_up_weight), squares, projected).reshape(8, rows // 8, -1)
    own_b = jnp.pad(factor_b, ((0, 0), (0, LANES)))
    sent = jnp.concatenate([sent, jnp.broadcast_to(own_b[None], (8,) + own_b.shape)], axis=1)
    near = exchange(sent, "src", NEAR)
    near_sum = total(near[:, : rows // 8])
    near_b = near[:, rows // 8 :].reshape(-1, units + LANES)
    values, squares = unpack(near_sum, units)
    projected = near_sum[:, units + 3 : units + 3 + ranks]
    sent = jnp.concatenate([pack(values, squares, projected), near_b], axis=0)
    far = share(sent, "src", FAR, 4)
    far_sum = total(far[:, : rows // 8])
    ranks_b = far[:, rows // 8 :, :units].reshape(ranks, units)
    values, squares = unpack(far_sum, units)
    projected = far_sum[:, units + 3 : units + 3 + ranks]
    high = lax.reduce_precision(projected, 8, 7)
    both = jnp.concatenate([high, projected - high], axis=0).astype(jnp.bfloat16)
    update = dot(both, ranks_b)
    update = update[: rows // 8] + update[rows // 8 :]
    active = activate(values + ADAPTER_SCALING * update, squares)

    low_rank_update = lax.dot_general(
        ranks_a, ranks_b, (((0,), (0,)), ((), ())), preferred_element_type=jnp.float32
    )
    up_own = (
        frozen_up_weight.astype(jnp.float32) + ADAPTER_SCALING * low_rank_update
    ).astype(jnp.bfloat16)
    up_other = lax.ppermute(up_own, "tp", SWAP)

    sent = jnp.broadcast_to(
        active.reshape(2, 1, rows // 16, units), (2, 8, rows // 16, units)
    ).reshape(16, rows // 16, units)
    active = exchange(sent, ("src", "tp"), PAIRS).reshape(2, half, units)
    active_own = jnp.where(first, active[0], active[1])
    active_other = jnp.where(first, active[1], active[0])
    current = jnp.where(first, stream[:half], stream[half:])

    for step in range(STEPS):
        if step > 0:
            squares = jnp.sum(current * current, axis=1, keepdims=True)
            scaled = (current * norm_gain).astype(jnp.bfloat16)
            values = jnp.concatenate([dot(scaled, up_own), dot(scaled, up_other)], axis=1)
            sent = pack(values, squares).reshape(8, half // 8, -1)
            near = total(exchange(sent, "src", NEAR))
            far = total(share(pack(*unpack(near, 2 * units)), "src", FAR, 4))
            active = activate(*unpack(far, 2 * units))
            active = share(active, "src", NEAR, 8).reshape(half, 2 * units)
            active_own, active_other = active[:, :units], active[:, units:]
        branch = dot(active_own, down_own) + dot(active_other, down_other)
        current = current + total(share(branch.astype(jnp.bfloat16), "tp", CHIPS, 8))
    return share(current, "tp", CORES, 2).reshape(rows, width)


def solution(mesh):
    in_specs = (
        P(None, "src"),
        P("src"),
        P("src", "tp"),
        P("tp", "src"),
        P("src", "tp"),
        P("tp", "src"),
    )
    out_specs = P(None, "src")
    return jax.shard_map(
        per_device, mesh=mesh, in_specs=in_specs, out_specs=out_specs, check_vma=False
    )
```

time: 1320 us -> 233 us (0.18)
  waiting for transfers between devices: 1060 us -> 18.2 us
  blocking collectives: 231 us -> 139 us
  starting transfers between devices: 0.21 us -> 36.9 us
    psum x6 -> x0, waiting for transfers between devices: 1060 us -> none  [the longest x3 555 us: per_device(): combined_output, squares = lax.psum((partial_up, local_squares), 'src')]
    psum x3 -> x0, blocking collectives: 150 us -> none  [per_device(): combined_output, squares = lax.psum((partial_up, local_squares), 'src')]
    all_to_all x0 -> x11, blocking collectives: none -> 139 us  [exchange(): lax.all_to_all(blocks, axis, 0, 0, axis_index_groups=groups, tiled=True)]
    all_gather x2 -> x0, blocking collectives: 81.5 us -> none  [the longest x1 55.2 us: per_device(): ranks_b = lax.all_gather(factor_b, 'src', axis=0, tiled=True)]
    all_to_all x0 -> x3, starting transfers between devices: none -> 31 us  [exchange(): lax.all_to_all(blocks, axis, 0, 0, axis_index_groups=groups, tiled=True)]
    all_to_all x0 -> x3, waiting for transfers between devices: none -> 18.2 us  [exchange(): lax.all_to_all(blocks, axis, 0, 0, axis_index_groups=groups, tiled=True)]
  transfers between devices with their start and end apart: 6 -> 5, of which waited for: 6 -> 2; matrix products, arithmetic and copies ran while one was open for 0% -> 8% of each run, Pallas kernels for 0% -> 0%
where the time goes in v2:
time: 233 us; the launch traced here: 232 us
  blocking collectives  139 us (60%)
  starting transfers between devices  36.9 us (16%)
  matrix products  21.1 us (9%)
  waiting for transfers between devices  18.2 us (8%)
  local copies, waits for them, and re-layouts  12.8 us (5%)
  other arithmetic  3.6 us (2%)
    all_to_all x11, blocking collectives, exchange(): lax.all_to_all(blocks, axis, 0, 0, axis_index_groups=groups, tiled=True)  139 us
    all_to_all x3, starting transfers between devices, exchange(): lax.all_to_all(blocks, axis, 0, 0, axis_index_groups=groups, tiled=True)  31 us
    all_to_all x3, waiting for transfers between devices, exchange(): lax.all_to_all(blocks, axis, 0, 0, axis_index_groups=groups, tiled=True)  18.2 us
    dot_general x12, matrix products, dot(): return jnp.dot(a, b, preferred_element_type=jnp.float32)  17.5 us
  transfers between devices with their start and end apart: 5, of which 2 were waited for; matrix products, arithmetic and copies ran while one was open for 8% of the time, Pallas kernels for 0%

profile of v2, /device:TPU:1, one launch (start us, length us, event | category | flops | bytes accessed | tf_op | source)
XLA Modules:
  0.0 231.6 jit_solution(8165385700652602160)
XLA Ops:
  0.0 1.3 broadcast_in_dim.30
  1.4 10.2 %all-to-all-start = ((bf16[16,4,512]{2,1,0:T(4,128)(2,1)}), bf16[16,4,512]{2,1,0:T(4,128)(2,1)S(1)}, u32[]{:S(2)}, u32[]{:S(2)}) async-start(bf16[16,4,512]{2,1,0:T(4,128)(2,1)} %broadcast_in_dim.30), calls=%async_computation | async-start | bytes 131072 | tf_op jit(solution)/shard_map/all_to_all | solution.py:26
  11.5 0.9 reshape.390
  12.5 0.8 fusion.6
  13.3 0.7 fusion.5
  14.1 1.9 convolution_convert_fusion
  16.5 2.5 %all-to-all-done = bf16[16,4,512]{2,1,0:T(4,128)(2,1)S(1)} async-done(((bf16[16,4,512]{2,1,0:T(4,128)(2,1)}), bf16[16,4,512]{2,1,0:T(4,128)(2,1)S(1)}, u32[]{:S(2)}, u32[]{:S(2)}) %all-to-all-start) | async-done | bytes 65568 | tf_op jit(solution)/shard_map/all_to_all | solution.py:26
  19.1 0.2 convolution_convert_fusion.5
  19.5 17.8 %all_to_all.70 = bf16[8,10,1920]{2,1,0:T(8,128)(2,1)S(1)} all-to-all(bf16[8,10,1920]{2,1,0:T(8,128)(2,1)S(1)} %pad_maximum_fusion), channel_id=1, replica_groups={{0,16,32,48,256,272,288,304},{64,80,96,112,320,336,352,368},{128,144,16..., dimensions={0} | all-to-all | bytes 614400 | tf_op jit(solution)/shard_map/all_to_all | solution.py:26
  38.0 0.8 broadcast_in_dim.34
  38.8 12.1 %all-to-all-start.2 = ((bf16[4,24,1920]{2,1,0:T(8,128)(2,1)}), bf16[4,24,1920]{2,1,0:T(8,128)(2,1)S(1)}, u32[]{:S(2)}, u32[]{:S(2)}) async-start(bf16[4,24,1920]{2,1,0:T(8,128)(2,1)} %broadcast_in_dim.34), calls=%async_computation.2 | async-start | bytes 737280 | tf_op jit(solution)/shard_map/all_to_all | solution.py:26
  50.9 3.9 %collective-permute-start = (bf16[1792,512]{1,0:T(8,128)(2,1)S(1)}, bf16[1792,512]{1,0:T(8,128)(2,1)}, u32[]{:S(2)}, u32[]{:S(2)}) collective-permute-start(bf16[1792,512]{1,0:T(8,128)(2,1)S(1)} %copy-done), channel_id=1, source_target_pairs={{0,1},{1,0},{2,3},{3,2},{4,5},{5,4},{6,7},{7,6},{8,9},{9,8},{10,11... | collective-permute-start | bytes 5505032 | tf_op jit(solution)/shard_map/ppermute | solution.py:71
  54.8 15.7 %all-to-all-done.2 = bf16[4,24,1920]{2,1,0:T(8,128)(2,1)S(1)} async-done(((bf16[4,24,1920]{2,1,0:T(8,128)(2,1)}), bf16[4,24,1920]{2,1,0:T(8,128)(2,1)S(1)}, u32[]{:S(2)}, u32[]{:S(2)}) %all-to-all-start.2) | async-done | bytes 368672 | tf_op jit(solution)/shard_map/all_to_all | solution.py:26
  70.8 0.1 fusion.25
  71.0 0.8 broadcast_in_dim.36
  71.8 8.7 %all-to-all-start.3 = ((bf16[16,4,1792]{2,1,0:T(4,128)(2,1)}), bf16[16,4,1792]{2,1,0:T(4,128)(2,1)S(1)}, u32[]{:S(2)}, u32[]{:S(2)}) async-start(bf16[16,4,1792]{2,1,0:T(4,128)(2,1)} %bitcast.8), calls=%async_computation.3 | async-start | bytes 458752 | tf_op jit(solution)/shard_map/all_to_all | solution.py:26
  80.5 3.8 %copy.153 = bf16[512,1792]{0,1:T(8,128)(2,1)} copy(bf16[512,1792]{1,0:T(8,128)(2,1)} %param.8) | data formatting | bytes 3670016 | tf_op args[2]
  84.4 3.4 %fusion = bf16[512,1792]{0,1:T(8,128)(2,1)} fusion(bf16[512,1792]{0,1:T(8,128)(2,1)} %copy.153, bf16[64,1792]{1,0:T(8,128)(2,1)S(1)} %bitcast.63, bf16[64,512]{1,0:T(8,128)(2,1)S(1)} %reshape.393), kind=kOutput, calls=%fused_computation.1 | convolution fusion | flops 121110528 | bytes 3964928 | tf_op jit(solution)/shard_map/dot_general | solution.py:103
  87.8 2.0 collective-permute-start.1
  90.0 0.4 fusion.33
  90.4 1.9 fusion.2
  92.4 12.0 %all_to_all.71 = bf16[8,32,512]{2,1,0:T(8,128)(2,1)S(1)} all-to-all(bf16[8,32,512]{2,1,0:T(8,128)(2,1)S(1)} %broadcast_in_dim.37), channel_id=1, replica_groups={{0,2,4,6,8,10,12,14},{1,3,5,7,9,11,13,15},{16,18,20,22,24,26,28,30},{17..., dimensions={0} | all-to-all | bytes 524288 | tf_op jit(solution)/shard_map/all_to_all | solution.py:26
  104.6 0.2 copy.156
  104.8 0.1 copy.155
  104.9 0.1 copy.154
  105.1 2.1 convolution_convert_fusion.4
  107.3 2.1 convolution_convert_fusion.3
  109.5 0.2 concatenate.65
  109.7 12.4 %all_to_all.72 = bf16[8,4,3712]{2,1,0:T(4,128)(2,1)S(1)} all-to-all(bf16[8,4,3712]{2,1,0:T(4,128)(2,1)S(1)} %concatenate.65), channel_id=1, replica_groups={{0,16,32,48,256,272,288,304},{64,80,96,112,320,336,352,368},{128,144,16..., dimensions={0} | all-to-all | bytes 475136 | tf_op jit(solution)/shard_map/all_to_all | solution.py:26
  122.9 14.7 %all_to_all.73 = bf16[4,4,3712]{2,1,0:T(4,128)(2,1)S(1)} all-to-all(bf16[4,4,3712]{2,1,0:T(4,128)(2,1)S(1)} %broadcast_in_dim.38), channel_id=1, replica_groups={{0,64,128,192},{16,80,144,208},{32,96,160,224},{48,112,176,240},{256,32..., dimensions={0} | all-to-all | bytes 237568 | tf_op jit(solution)/shard_map/all_to_all | solution.py:26
  138.0 10.5 %all_to_all.74 = bf16[8,4,3584]{2,1,0:T(4,128)(2,1)S(1)} all-to-all(bf16[8,4,3584]{2,1,0:T(4,128)(2,1)S(1)} %broadcast_in_dim.39), channel_id=1, replica_groups={{0,16,32,48,256,272,288,304},{64,80,96,112,320,336,352,368},{128,144,16..., dimensions={0} | all-to-all | bytes 458752 | tf_op jit(solution)/shard_map/all_to_all | solution.py:26
  148.5 0.4 fusion.12
  148.9 1.9 fusion.3
  150.9 12.2 %all_to_all.75 = bf16[8,32,512]{2,1,0:T(8,128)(2,1)S(1)} all-to-all(bf16[8,32,512]{2,1,0:T(8,128)(2,1)S(1)} %broadcast_in_dim.40), channel_id=1, replica_groups={{0,2,4,6,8,10,12,14},{1,3,5,7,9,11,13,15},{16,18,20,22,24,26,28,30},{17..., dimensions={0} | all-to-all | bytes 524288 | tf_op jit(solution)/shard_map/all_to_all | solution.py:26
  163.2 2.1 convolution_convert_fusion.2
  165.4 2.1 convolution_convert_fusion.1
  167.7 0.2 copy.162
  167.8 0.1 copy.161
  167.9 0.1 copy.160
  168.1 0.3 concatenate.70
  168.4 9.6 %all_to_all.76 = bf16[8,4,3712]{2,1,0:T(4,128)(2,1)S(1)} all-to-all(bf16[8,4,3712]{2,1,0:T(4,128)(2,1)S(1)} %concatenate.70), channel_id=1, replica_groups={{0,16,32,48,256,272,288,304},{64,80,96,112,320,336,352,368},{128,144,16..., dimensions={0} | all-to-all | bytes 475136 | tf_op jit(solution)/shard_map/all_to_all | solution.py:26
  178.7 14.7 %all_to_all.77 = bf16[4,4,3712]{2,1,0:T(4,128)(2,1)S(1)} all-to-all(bf16[4,4,3712]{2,1,0:T(4,128)(2,1)S(1)} %broadcast_in_dim.41), channel_id=1, replica_groups={{0,64,128,192},{16,80,144,208},{32,96,160,224},{48,112,176,240},{256,32..., dimensions={0} | all-to-all | bytes 237568 | tf_op jit(solution)/shard_map/all_to_all | solution.py:26
  193.8 9.6 %all_to_all.78 = bf16[8,4,3584]{2,1,0:T(4,128)(2,1)S(1)} all-to-all(bf16[8,4,3584]{2,1,0:T(4,128)(2,1)S(1)} %broadcast_in_dim.42), channel_id=1, replica_groups={{0,16,32,48,256,272,288,304},{64,80,96,112,320,336,352,368},{128,144,16..., dimensions={0} | all-to-all | bytes 458752 | tf_op jit(solution)/shard_map/all_to_all | solution.py:26
  203.5 0.4 fusion.9
  203.9 1.9 fusion.4
  205.8 10.2 %all_to_all.79 = bf16[8,32,512]{2,1,0:T(8,128)(2,1)S(1)} all-to-all(bf16[8,32,512]{2,1,0:T(8,128)(2,1)S(1)} %broadcast_in_dim.43), channel_id=1, replica_groups={{0,2,4,6,8,10,12,14},{1,3,5,7,9,11,13,15},{16,18,20,22,24,26,28,30},{17..., dimensions={0} | all-to-all | bytes 524288 | tf_op jit(solution)/shard_map/all_to_all | solution.py:26
  216.2 14.8 %all_to_all.80 = f32[2,32,512]{2,1,0:T(8,128)S(1)} all-to-all(f32[2,32,512]{2,1,0:T(8,128)S(1)} %broadcast_in_dim.44), channel_id=1, replica_groups={{0,1},{2,3},{4,5},{6,7},{8,9},{10,11},{12,13},{14,15},{16,17},{18,19},{..., dimensions={0} | all-to-all | bytes 262144 | tf_op jit(solution)/shard_map/all_to_all | solution.py:26
  231.0 0.7 copy.174
  (100 shorter events, 5.2 us)
Async XLA Ops:
  0.0 16.4 %copy-start.3 = (bf16[2,1792]{1,0:T(2,128)(2,1)S(1)}, bf16[2,1792]{1,0:T(2,128)(2,1)}, u32[]{:S(2)}) copy-start(bf16[2,1792]{1,0:T(2,128)(2,1)} %param.10) | copy-start | bytes 21508
  1.4 17.6 %all-to-all-start = ((bf16[16,4,512]{2,1,0:T(4,128)(2,1)}), bf16[16,4,512]{2,1,0:T(4,128)(2,1)S(1)}, u32[]{:S(2)}, u32[]{:S(2)}) async-start(bf16[16,4,512]{2,1,0:T(4,128)(2,1)} %broadcast_in_dim.30), calls=%async_computation | async-start | bytes 131072 | tf_op jit(solution)/shard_map/all_to_all | solution.py:26
  19.4 31.5 %copy-start = (bf16[1792,512]{1,0:T(8,128)(2,1)S(1)}, bf16[1792,512]{1,0:T(8,128)(2,1)}, u32[]{:S(2)}) copy-start(bf16[1792,512]{1,0:T(8,128)(2,1)} %param.11) | copy-start | bytes 5505028
  38.8 31.7 %all-to-all-start.2 = ((bf16[4,24,1920]{2,1,0:T(8,128)(2,1)}), bf16[4,24,1920]{2,1,0:T(8,128)(2,1)S(1)}, u32[]{:S(2)}, u32[]{:S(2)}) async-start(bf16[4,24,1920]{2,1,0:T(8,128)(2,1)} %broadcast_in_dim.34), calls=%async_computation.2 | async-start | bytes 737280 | tf_op jit(solution)/shard_map/all_to_all | solution.py:26
  50.9 39.5 %collective-permute-start = (bf16[1792,512]{1,0:T(8,128)(2,1)S(1)}, bf16[1792,512]{1,0:T(8,128)(2,1)}, u32[]{:S(2)}, u32[]{:S(2)}) collective-permute-start(bf16[1792,512]{1,0:T(8,128)(2,1)S(1)} %copy-done), channel_id=1, source_target_pairs={{0,1},{1,0},{2,3},{3,2},{4,5},{5,4},{6,7},{7,6},{8,9},{9,8},{10,11... | collective-permute-start | bytes 5505032 | tf_op jit(solution)/shard_map/ppermute | solution.py:71
  71.8 18.0 %all-to-all-start.3 = ((bf16[16,4,1792]{2,1,0:T(4,128)(2,1)}), bf16[16,4,1792]{2,1,0:T(4,128)(2,1)S(1)}, u32[]{:S(2)}, u32[]{:S(2)}) async-start(bf16[16,4,1792]{2,1,0:T(4,128)(2,1)} %bitcast.8), calls=%async_computation.3 | async-start | bytes 458752 | tf_op jit(solution)/shard_map/all_to_all | solution.py:26
  87.8 19.5 %collective-permute-start.1 = (bf16[512,1792]{0,1:T(8,128)(2,1)}, bf16[512,1792]{0,1:T(8,128)(2,1)}, u32[]{:S(2)}, u32[]{:S(2)}) collective-permute-start(bf16[512,1792]{0,1:T(8,128)(2,1)} %fusion), channel_id=1, source_target_pairs={{0,1},{1,0},{2,3},{3,2},{4,5},{5,4},{6,7},{7,6},{8,9},{9,8},{10,11... | collective-permute-start | bytes 5505032 | tf_op jit(solution)/shard_map/ppermute | solution.py:109
  90.4 14.0 %copy-start.1 = (f32[64,512]{1,0:T(8,128)S(1)}, f32[64,512]{1,0:T(8,128)}, u32[]{:S(2)}) copy-start(f32[64,512]{1,0:T(8,128)} %param.6) | copy-start | bytes 393220
  90.4 14.7 %copy-start.2 = (f32[512]{0:T(512)S(1)}, f32[512]{0:T(512)}, u32[]{:S(2)}) copy-start(f32[512]{0:T(512)} %param.7) | copy-start | bytes 6148

commit v3 on v2

v3 whole, which is shorter than its diff:
```python
import jax
import jax.numpy as jnp
from jax import lax
from jax.experimental import pallas as pl
from jax.experimental.pallas import tpu as pltpu
from jax.sharding import PartitionSpec as P

D = 16384
STEPS = 3
LANES = 128

ADAPTER_SCALING = 2.0
EPSILON = 1e-05

NEAR = [[y * 16 + far * 4 + low for y in range(2) for low in range(4)] for far in range(4)]
FAR = [[y * 16 + far * 4 + low for far in range(4)] for y in range(2) for low in range(4)]
PAIRS = [
    [src * 16 + chip * 2 + core for core in range(2) for src in near]
    for near in NEAR
    for chip in range(8)
]
CORES = [[2 * chip, 2 * chip + 1] for chip in range(8)]
CHIPS = [[2 * chip + core for chip in range(8)] for core in range(2)]
SWAP = [(i, i ^ 1) for i in range(16)]


def exchange(blocks, axis, groups):
    return lax.all_to_all(blocks, axis, 0, 0, axis_index_groups=groups, tiled=True)


def share(block, axis, groups, size):
    return exchange(jnp.broadcast_to(block[None], (size,) + block.shape), axis, groups)


def total(blocks):
    return jnp.sum(blocks.astype(jnp.float32), axis=0)


def pack(values, squares, others=None):
    high = lax.reduce_precision(squares, 8, 7)
    rest = squares - high
    middle = lax.reduce_precision(rest, 8, 7)
    parts = [values, high, middle, rest - middle]
    used = 3
    if others is not None:
        parts.append(others)
        used += others.shape[1]
    parts.append(jnp.zeros((values.shape[0], LANES - used), jnp.float32))
    return jnp.concatenate(parts, axis=1).astype(jnp.bfloat16)


def unpack(both, width):
    return both[:, :width], jnp.sum(both[:, width : width + 3], axis=1, keepdims=True)


def activate(values, squares):
    hidden = values * lax.rsqrt(squares / D + EPSILON)
    return jax.nn.silu(hidden).astype(jnp.bfloat16)


def dot(a, b):
    return jnp.dot(a, b, preferred_element_type=jnp.float32)


def params():
    return pltpu.CompilerParams(vmem_limit_bytes=24 * 1024 * 1024)


VMEM = pl.BlockSpec(memory_space=pltpu.VMEM)
ANYWHERE = pl.BlockSpec(memory_space=pl.ANY)


def merge_kernel(up_ref, a_ref, b_ref, out_ref):
    update = dot(a_ref[...], b_ref[...])
    out_ref[...] = (
        up_ref[...].astype(jnp.float32) + ADAPTER_SCALING * update
    ).astype(jnp.bfloat16)


def merge(up, ranks_a, ranks_b):
    width, units = up.shape
    ranks = ranks_b.shape[0]
    block = units // 2
    return pl.pallas_call(
        merge_kernel,
        grid=(units // block,),
        in_specs=[
            pl.BlockSpec((width, block), lambda i: (0, i)),
            pl.BlockSpec((width, ranks), lambda i: (0, 0)),
            pl.BlockSpec((ranks, block), lambda i: (0, i)),
        ],
        out_specs=pl.BlockSpec((width, block), lambda i: (0, i)),
        out_shape=jax.ShapeDtypeStruct(up.shape, jnp.bfloat16),
        compiler_params=params(),
        cost_estimate=pl.CostEstimate(
            flops=2 * width * units * ranks, bytes_accessed=4 * width * units, transcendentals=0
        ),
    )(up, ranks_a.T, ranks_b)


def up_kernel(branch_ref, current_ref, gain_ref, own_ref, other_ref, next_ref, sent_ref, held, sems):
    units = own_ref.shape[1]
    part = units // 2
    copies = []
    for i in range(4):
        source = (own_ref, other_ref)[i // 2].at[:, pl.ds((i % 2) * part, part)]
        copies.append(pltpu.make_async_copy(source, held.at[i], sems.at[i]))
        copies[-1].start()
    current = current_ref[...] + jnp.sum(branch_ref[...].astype(jnp.float32), axis=0)
    next_ref[...] = current
    scaled = (current * gain_ref[...]).astype(jnp.bfloat16)
    squares = jnp.sum(current * current, axis=1, keepdims=True)
    high = squares.astype(jnp.bfloat16).astype(jnp.float32)
    rest = squares - high
    middle = rest.astype(jnp.bfloat16).astype(jnp.float32)
    lane = lax.broadcasted_iota(jnp.int32, (current.shape[0], LANES), 1)
    tail = jnp.where(lane == 0, high, jnp.where(lane == 1, middle, rest - middle))
    sent_ref[:, pl.ds(2 * units, LANES)] = jnp.where(lane < 3, tail, 0.0).astype(jnp.bfloat16)
    for i in range(4):
        copies[i].wait()
        sent_ref[:, pl.ds(i * part, part)] = dot(scaled, held[i]).astype(jnp.bfloat16)


def up(branches, current, gain, own, other):
    rows, width = current.shape
    units = own.shape[1]
    return pl.pallas_call(
        up_kernel,
        in_specs=[VMEM, VMEM, VMEM, ANYWHERE, ANYWHERE],
        out_specs=[VMEM, VMEM],
        out_shape=[
            jax.ShapeDtypeStruct(current.shape, jnp.float32),
            jax.ShapeDtypeStruct((rows, 2 * units + LANES), jnp.bfloat16),
        ],
        scratch_shapes=[
            pltpu.VMEM((4, width, units // 2), jnp.bfloat16),
            pltpu.SemaphoreType.DMA((4,)),
        ],
        compiler_params=params(),
        cost_estimate=pl.CostEstimate(
            flops=4 * rows * width * units, bytes_accessed=4 * width * units, transcendentals=0
        ),
    )(branches, current, gain, own, other)


def down_kernel(active_ref, own_ref, other_ref, out_ref, held, sems):
    part = own_ref.shape[0] // 2
    copies = []
    for i in range(4):
        source = (own_ref, other_ref)[i // 2].at[pl.ds((i % 2) * part, part)]
        copies.append(pltpu.make_async_copy(source, held.at[i], sems.at[i]))
        copies[-1].start()
    branch = jnp.zeros(out_ref.shape[1:], jnp.float32)
    for i in range(4):
        copies[i].wait()
        branch = branch + dot(active_ref[:, pl.ds(i * part, part)], held[i])
    out_ref[...] = jnp.broadcast_to(branch.astype(jnp.bfloat16)[None], out_ref.shape)


def down(active, own, other, copies):
    rows = active.shape[0]
    units, width = own.shape
    return pl.pallas_call(
        down_kernel,
        in_specs=[VMEM, ANYWHERE, ANYWHERE],
        out_specs=VMEM,
        out_shape=jax.ShapeDtypeStruct((copies, rows, width), jnp.bfloat16),
        scratch_shapes=[
            pltpu.VMEM((4, units // 2, width), jnp.bfloat16),
            pltpu.SemaphoreType.DMA((4,)),
        ],
        compiler_params=params(),
        cost_estimate=pl.CostEstimate(
            flops=4 * rows * width * units, bytes_accessed=4 * width * units, transcendentals=0
        ),
    )(active, own, other)


def per_device(stream, norm_gain, frozen_up_weight, factor_a, factor_b, down_projection_matrix):
    rows, width = stream.shape
    units = frozen_up_weight.shape[1]
    half = rows // 2
    first = lax.axis_index("tp") % 2 == 0
    gain = norm_gain[None]

    ranks_a = share(factor_a, "tp", None, 16)
    ranks_a = ranks_a.reshape(2, 4, 4, 2, width).transpose(1, 0, 2, 3, 4).reshape(-1, width)
    ranks = ranks_a.shape[0]

    ordered = stream.reshape(2, 8, rows // 16, width).transpose(1, 0, 2, 3).reshape(rows, width)
    scaled = (ordered * gain).astype(jnp.bfloat16)
    squares = jnp.sum(ordered * ordered, axis=1, keepdims=True)
    projected = lax.dot_general(
        scaled, ranks_a, (((1,), (1,)), ((), ())), preferred_element_type=jnp.float32
    )
    sent = pack(dot(scaled, frozen_up_weight), squares, projected).reshape(8, rows // 8, -1)
    end = sent.shape[2]
    own_b = jnp.pad(factor_b.reshape(8, units // 4), ((0, 0), (0, 512 - units // 4)))
    sent = jnp.concatenate([sent, jnp.broadcast_to(own_b[None], (8,) + own_b.shape)], axis=2)
    near = exchange(sent, "src", NEAR)
    near_sum = total(near[:, :, :end])
    values, squares = unpack(near_sum, units)
    projected = near_sum[:, units + 3 : units + 3 + ranks]
    sent = jnp.concatenate(
        [pack(values, squares, projected)] + [near[i, :, end:] for i in range(8)], axis=1
    )
    far = share(sent, "src", FAR, 4)
    far_sum = total(far[:, :, :end])
    ranks_b = far[:, :, end:].reshape(4, 8, 8, 512)[..., : units // 4]
    ranks_b = ranks_b.transpose(0, 2, 1, 3).reshape(ranks, units)
    values, squares = unpack(far_sum, units)
    projected = far_sum[:, units + 3 : units + 3 + ranks]
    high = lax.reduce_precision(projected, 8, 7)
    both = jnp.concatenate([high, projected - high], axis=0).astype(jnp.bfloat16)
    update = dot(both, ranks_b)
    update = update[: rows // 8] + update[rows // 8 :]
    active = activate(values + ADAPTER_SCALING * update, squares)

    down_own = down_projection_matrix
    down_other = lax.ppermute(down_own, "tp", SWAP)
    up_own = merge(frozen_up_weight, ranks_a, ranks_b)
    up_other = lax.ppermute(up_own, "tp", SWAP)

    sent = jnp.broadcast_to(
        active.reshape(2, 1, rows // 16, units), (2, 8, rows // 16, units)
    ).reshape(16, rows // 16, units)
    active = exchange(sent, ("src", "tp"), PAIRS).reshape(2, half, units)
    active = jnp.concatenate(
        [jnp.where(first, active[0], active[1]), jnp.where(first, active[1], active[0])], axis=1
    )
    current = jnp.where(first, stream[:half], stream[half:])
    branches = exchange(down(active, down_own, down_other, 8), "tp", CHIPS)

    for step in range(1, STEPS):
        current, sent = up(branches, current, gain, up_own, up_other)
        near = total(exchange(sent.reshape(8, half // 8, -1), "src", NEAR))
        far = total(share(pack(*unpack(near, 2 * units)), "src", FAR, 4))
        active = activate(*unpack(far, 2 * units))
        active = share(active, "src", NEAR, 8).reshape(half, 2 * units)
        branches = exchange(down(active, down_own, down_other, 8), "tp", CHIPS)
    current = current + total(branches)
    return share(current, "tp", CORES, 2).reshape(rows, width)


def solution(mesh):
    in_specs = (
        P(None, "src"),
        P("src"),
        P("src", "tp"),
        P("tp", "src"),
        P("src", "tp"),
        P("tp", "src"),
    )
    out_specs = P(None, "src")
    return jax.shard_map(
        per_device, mesh=mesh, in_specs=in_specs, out_specs=out_specs, check_vma=False
    )
```

time: 233 us -> 223 us (0.957)
  blocking collectives: 139 us -> 119 us
  matrix products: 21.1 us -> 2.21 us
  waiting for transfers between devices: 18.2 us -> 32.2 us
  Pallas kernels: 0 us -> 12.8 us
  starting transfers between devices: 36.9 us -> 42.5 us
  local copies, waits for them, and re-layouts: 12.8 us -> 9.13 us
    all_to_all x11 -> x10, blocking collectives: 139 us -> 119 us  [exchange(): lax.all_to_all(blocks, axis, 0, 0, axis_index_groups=groups, tiled=True)]
    dot_general x12 -> x2, matrix products: 17.5 us -> 2.06 us  [dot(): return jnp.dot(a, b, preferred_element_type=jnp.float32)]
    all_to_all x3 -> x4, waiting for transfers between devices: 18.2 us -> 32.2 us  [exchange(): lax.all_to_all(blocks, axis, 0, 0, axis_index_groups=groups, tiled=True)]
    pallas_call x0 -> x6, Pallas kernels: none -> 12.8 us  [the longest x3 7.72 us: down(): pl.pallas_call(down_kernel, in_specs=[VMEM, ANYWHERE, ANYWHERE], out_spec...]
    all_to_all x3 -> x4, starting transfers between devices: 31 us -> 35.7 us  [exchange(): lax.all_to_all(blocks, axis, 0, 0, axis_index_groups=groups, tiled=True)]
    dot_general x1 -> x0, matrix products: 3.42 us -> none  [per_device(): lax.dot_general(ranks_a, ranks_b, (((0,), (0,)), ((), ())), preferred_ele...]
    unnamed x10 -> x9, local copies, waits for them, and re-layouts: 4.51 us -> 2.17 us
  transfers between devices with their start and end apart: 5 -> 6, of which waited for: 2 -> 4; matrix products, arithmetic and copies ran while one was open for 8% -> 3% of each run, Pallas kernels for 0% -> 2%
where the time goes in v3:
time: 223 us; the launch traced here: 222 us
  blocking collectives  119 us (53%)
  starting transfers between devices  42.5 us (19%)
  waiting for transfers between devices  32.2 us (14%)
  Pallas kernels  12.8 us (6%)
  local copies, waits for them, and re-layouts  9.13 us (4%)
  other arithmetic  3.22 us (1%)
    all_to_all x10, blocking collectives, exchange(): lax.all_to_all(blocks, axis, 0, 0, axis_index_groups=groups, tiled=True)  119 us
    all_to_all x4, starting transfers between devices, exchange(): lax.all_to_all(blocks, axis, 0, 0, axis_index_groups=groups, tiled=True)  35.7 us
    all_to_all x4, waiting for transfers between devices, exchange(): lax.all_to_all(blocks, axis, 0, 0, axis_index_groups=groups, tiled=True)  32.2 us
    pallas_call x3, Pallas kernels, down(): pl.pallas_call(down_kernel, in_specs=[VMEM, ANYWHERE, ANYWHERE], out_spec...  7.72 us
    ppermute x1, starting transfers between devices, per_device(): down_other = lax.ppermute(down_own, 'tp', SWAP)  4.79 us
  transfers between devices with their start and end apart: 6, of which 4 were waited for; matrix products, arithmetic and copies ran while one was open for 3% of the time, Pallas kernels for 2%

profile of v3, /device:TPU:1, one launch (start us, length us, event | category | flops | bytes accessed | tf_op | source)
XLA Modules:
  0.0 221.5 jit_solution(4461328278833602968)
XLA Ops:
  0.0 1.3 broadcast_in_dim.26
  1.4 10.2 %all-to-all-start = ((bf16[16,4,512]{2,1,0:T(4,128)(2,1)}), bf16[16,4,512]{2,1,0:T(4,128)(2,1)S(1)}, u32[]{:S(2)}, u32[]{:S(2)}) async-start(bf16[16,4,512]{2,1,0:T(4,128)(2,1)} %broadcast_in_dim.26), calls=%async_computation | async-start | bytes 131072 | tf_op jit(solution)/shard_map/all_to_all | solution.py:28
  11.5 0.9 reshape.300
  12.5 0.8 fusion.2
  13.3 0.7 fusion.1
  14.1 1.9 convolution_convert_fusion
  16.1 0.1 copy.138
  16.3 0.1 copy.137
  16.4 0.1 copy.136
  16.5 2.4 %all-to-all-done = bf16[16,4,512]{2,1,0:T(4,128)(2,1)S(1)} async-done(((bf16[16,4,512]{2,1,0:T(4,128)(2,1)}), bf16[16,4,512]{2,1,0:T(4,128)(2,1)S(1)}, u32[]{:S(2)}, u32[]{:S(2)}) %all-to-all-start) | async-done | bytes 65568 | tf_op jit(solution)/shard_map/all_to_all | solution.py:28
  19.1 0.2 convolution_convert_fusion.1
  19.4 12.9 %all_to_all.70 = bf16[8,8,2432]{2,1,0:T(8,128)(2,1)S(1)} all-to-all(bf16[8,8,2432]{2,1,0:T(8,128)(2,1)S(1)} %concatenate.38), channel_id=1, replica_groups={{0,16,32,48,256,272,288,304},{64,80,96,112,320,336,352,368},{128,144,16..., dimensions={0} | all-to-all | bytes 622592 | tf_op jit(solution)/shard_map/all_to_all | solution.py:28
  32.3 0.1 slice_reduce_fusion.1
  32.9 0.8 broadcast_in_dim.30
  33.7 12.1 %all-to-all-start.2 = ((bf16[4,8,6016]{2,1,0:T(8,128)(2,1)}), bf16[4,8,6016]{2,1,0:T(8,128)(2,1)S(1)}, u32[]{:S(2)}, u32[]{:S(2)}) async-start(bf16[4,8,6016]{2,1,0:T(8,128)(2,1)} %broadcast_in_dim.30), calls=%async_computation.2 | async-start | bytes 770048 | tf_op jit(solution)/shard_map/all_to_all | solution.py:28
  45.8 4.8 %collective-permute-start = (bf16[1792,512]{1,0:T(8,128)(2,1)}, bf16[1792,512]{1,0:T(8,128)(2,1)}, u32[]{:S(2)}, u32[]{:S(2)}) collective-permute-start(bf16[1792,512]{1,0:T(8,128)(2,1)} %own_ref.5), channel_id=1, source_target_pairs={{0,1},{1,0},{2,3},{3,2},{4,5},{5,4},{6,7},{7,6},{8,9},{9,8},{10,11... | collective-permute-start | bytes 5505032 | tf_op jit(solution)/shard_map/ppermute | solution.py:220
  50.6 17.2 %all-to-all-done.2 = bf16[4,8,6016]{2,1,0:T(8,128)(2,1)S(1)} async-done(((bf16[4,8,6016]{2,1,0:T(8,128)(2,1)}), bf16[4,8,6016]{2,1,0:T(8,128)(2,1)S(1)}, u32[]{:S(2)}, u32[]{:S(2)}) %all-to-all-start.2) | async-done | bytes 385056 | tf_op jit(solution)/shard_map/all_to_all | solution.py:28
  68.1 0.3 reshape.306.b_ref
  68.4 0.1 fusion.13
  68.7 0.8 broadcast_in_dim.32
  69.4 8.5 %all-to-all-start.3 = ((bf16[16,4,1792]{2,1,0:T(4,128)(2,1)}), bf16[16,4,1792]{2,1,0:T(4,128)(2,1)S(1)}, u32[]{:S(2)}, u32[]{:S(2)}) async-start(bf16[16,4,1792]{2,1,0:T(4,128)(2,1)} %bitcast.17), calls=%async_computation.3 | async-start | bytes 458752 | tf_op jit(solution)/shard_map/all_to_all | solution.py:28
  78.0 0.1 copy.143
  78.1 1.5 copy-done
  79.6 1.1 shard_map.65.own_ref
  80.7 2.0 collective-permute-start.1
  82.8 4.4 %all-to-all-done.3 = bf16[16,4,1792]{2,1,0:T(4,128)(2,1)S(1)} async-done(((bf16[16,4,1792]{2,1,0:T(4,128)(2,1)}), bf16[16,4,1792]{2,1,0:T(4,128)(2,1)S(1)}, u32[]{:S(2)}, u32[]{:S(2)}) %all-to-all-start.3) | async-done | bytes 229408 | tf_op jit(solution)/shard_map/all_to_all | solution.py:28
  87.4 3.1 %shard_map.64 = bf16[8,32,512]{2,1,0:T(8,128)(2,1)} custom-call(bf16[32,3584]{1,0:T(8,128)(2,1)S(1)} %pad_maximum_fusion.active_ref, bf16[1792,512]{1,0:T(8,128)(2,1)} %own_ref.5, bf16[1792,512]{1,0:T(8,128)(2,1)} %collective-permute-done.other_ref), custom_call_target="tpu_custom_call" | custom-call | flops 117440512 | bytes 3670016 | tf_op jit(solution)/shard_map/pallas_call | solution.py:163
  90.5 4.9 %all-to-all-start.4 = ((bf16[8,32,512]{2,1,0:T(8,128)(2,1)}), bf16[8,32,512]{2,1,0:T(8,128)(2,1)S(1)}, u32[]{:S(2)}, u32[]{:S(2)}) async-start(bf16[8,32,512]{2,1,0:T(8,128)(2,1)} %shard_map.64), calls=%async_computation.4 | async-start | bytes 524288 | tf_op jit(solution)/shard_map/all_to_all | solution.py:28
  95.4 8.1 %all-to-all-done.4.branch_ref = bf16[8,32,512]{2,1,0:T(8,128)(2,1)S(1)} async-done(((bf16[8,32,512]{2,1,0:T(8,128)(2,1)}), bf16[8,32,512]{2,1,0:T(8,128)(2,1)S(1)}, u32[]{:S(2)}, u32[]{:S(2)}) %all-to-all-start.4) | async-done | bytes 262176 | tf_op jit(solution)/shard_map/all_to_all | solution.py:28
  103.6 2.0 shard_map.66
  105.6 9.8 %all_to_all.71 = bf16[8,4,3712]{2,1,0:T(4,128)(2,1)S(1)} all-to-all(bf16[8,4,3712]{2,1,0:T(4,128)(2,1)S(1)} %reshape.308), channel_id=1, replica_groups={{0,16,32,48,256,272,288,304},{64,80,96,112,320,336,352,368},{128,144,16..., dimensions={0} | all-to-all | bytes 475136 | tf_op jit(solution)/shard_map/all_to_all | solution.py:28
  115.5 0.1 slice_reduce_fusion.5
  116.1 15.6 %all_to_all.72 = bf16[4,4,3712]{2,1,0:T(4,128)(2,1)S(1)} all-to-all(bf16[4,4,3712]{2,1,0:T(4,128)(2,1)S(1)} %broadcast_in_dim.34), channel_id=1, replica_groups={{0,64,128,192},{16,80,144,208},{32,96,160,224},{48,112,176,240},{256,32..., dimensions={0} | all-to-all | bytes 237568 | tf_op jit(solution)/shard_map/all_to_all | solution.py:28
  131.7 0.1 slice_reduce_fusion.4
  131.9 0.1 fusion.9
  132.1 10.6 %all_to_all.73 = bf16[8,4,3584]{2,1,0:T(4,128)(2,1)S(1)} all-to-all(bf16[8,4,3584]{2,1,0:T(4,128)(2,1)S(1)} %broadcast_in_dim.35), channel_id=1, replica_groups={{0,16,32,48,256,272,288,304},{64,80,96,112,320,336,352,368},{128,144,16..., dimensions={0} | all-to-all | bytes 458752 | tf_op jit(solution)/shard_map/all_to_all | solution.py:28
  142.7 2.3 %shard_map.67 = bf16[8,32,512]{2,1,0:T(8,128)(2,1)S(1)} custom-call(bf16[32,3584]{1,0:T(8,128)(2,1)S(1)} %reshape.309.active_ref, bf16[1792,512]{1,0:T(8,128)(2,1)} %own_ref.5, bf16[1792,512]{1,0:T(8,128)(2,1)} %collective-permute-done.other_ref), custom_call_target="tpu_custom_call" | custom-call | flops 117440512 | bytes 3670016 | tf_op jit(solution)/shard_map/pallas_call | solution.py:163
  145.1 10.9 %all_to_all.74.branch_ref = bf16[8,32,512]{2,1,0:T(8,128)(2,1)S(1)} all-to-all(bf16[8,32,512]{2,1,0:T(8,128)(2,1)S(1)} %shard_map.67), channel_id=1, replica_groups={{0,2,4,6,8,10,12,14},{1,3,5,7,9,11,13,15},{16,18,20,22,24,26,28,30},{17..., dimensions={0} | all-to-all | bytes 524288 | tf_op jit(solution)/shard_map/all_to_all | solution.py:28
  156.0 2.0 shard_map.68
  158.0 9.6 %all_to_all.75 = bf16[8,4,3712]{2,1,0:T(4,128)(2,1)S(1)} all-to-all(bf16[8,4,3712]{2,1,0:T(4,128)(2,1)S(1)} %reshape.310), channel_id=1, replica_groups={{0,16,32,48,256,272,288,304},{64,80,96,112,320,336,352,368},{128,144,16..., dimensions={0} | all-to-all | bytes 475136 | tf_op jit(solution)/shard_map/all_to_all | solution.py:28
  167.8 0.1 slice_reduce_fusion.3
  168.4 14.5 %all_to_all.76 = bf16[4,4,3712]{2,1,0:T(4,128)(2,1)S(1)} all-to-all(bf16[4,4,3712]{2,1,0:T(4,128)(2,1)S(1)} %broadcast_in_dim.36), channel_id=1, replica_groups={{0,64,128,192},{16,80,144,208},{32,96,160,224},{48,112,176,240},{256,32..., dimensions={0} | all-to-all | bytes 237568 | tf_op jit(solution)/shard_map/all_to_all | solution.py:28
  182.9 0.1 slice_reduce_fusion.2
  183.2 9.7 %all_to_all.77 = bf16[8,4,3584]{2,1,0:T(4,128)(2,1)S(1)} all-to-all(bf16[8,4,3584]{2,1,0:T(4,128)(2,1)S(1)} %broadcast_in_dim.37), channel_id=1, replica_groups={{0,16,32,48,256,272,288,304},{64,80,96,112,320,336,352,368},{128,144,16..., dimensions={0} | all-to-all | bytes 458752 | tf_op jit(solution)/shard_map/all_to_all | solution.py:28
  193.0 2.3 %shard_map.69 = bf16[8,32,512]{2,1,0:T(8,128)(2,1)S(1)} custom-call(bf16[32,3584]{1,0:T(8,128)(2,1)S(1)} %reshape.311.active_ref, bf16[1792,512]{1,0:T(8,128)(2,1)} %own_ref.5, bf16[1792,512]{1,0:T(8,128)(2,1)} %collective-permute-done.other_ref), custom_call_target="tpu_custom_call" | custom-call | flops 117440512 | bytes 3670016 | tf_op jit(solution)/shard_map/pallas_call | solution.py:163
  195.3 10.3 %all_to_all.78 = bf16[8,32,512]{2,1,0:T(8,128)(2,1)S(1)} all-to-all(bf16[8,32,512]{2,1,0:T(8,128)(2,1)S(1)} %shard_map.69), channel_id=1, replica_groups={{0,2,4,6,8,10,12,14},{1,3,5,7,9,11,13,15},{16,18,20,22,24,26,28,30},{17..., dimensions={0} | all-to-all | bytes 524288 | tf_op jit(solution)/shard_map/all_to_all | solution.py:28
  205.7 15.2 %all_to_all.79 = f32[2,32,512]{2,1,0:T(8,128)S(1)} all-to-all(f32[2,32,512]{2,1,0:T(8,128)S(1)} %broadcast_in_dim.38), channel_id=1, replica_groups={{0,1},{2,3},{4,5},{6,7},{8,9},{10,11},{12,13},{14,15},{16,17},{18,19},{..., dimensions={0} | all-to-all | bytes 262144 | tf_op jit(solution)/shard_map/all_to_all | solution.py:28
  220.9 0.7 copy.159
  (76 shorter events, 3.4 us)
Async XLA Ops:
  0.0 16.0 %copy-start.3 = (bf16[2,1792]{1,0:T(2,128)(2,1)S(1)}, bf16[2,1792]{1,0:T(2,128)(2,1)}, u32[]{:S(2)}) copy-start(bf16[2,1792]{1,0:T(2,128)(2,1)} %param.10) | copy-start | bytes 21508
  1.4 17.6 %all-to-all-start = ((bf16[16,4,512]{2,1,0:T(4,128)(2,1)}), bf16[16,4,512]{2,1,0:T(4,128)(2,1)S(1)}, u32[]{:S(2)}, u32[]{:S(2)}) async-start(bf16[16,4,512]{2,1,0:T(4,128)(2,1)} %broadcast_in_dim.26), calls=%async_computation | async-start | bytes 131072 | tf_op jit(solution)/shard_map/all_to_all | solution.py:28
  33.7 34.2 %all-to-all-start.2 = ((bf16[4,8,6016]{2,1,0:T(8,128)(2,1)}), bf16[4,8,6016]{2,1,0:T(8,128)(2,1)S(1)}, u32[]{:S(2)}, u32[]{:S(2)}) async-start(bf16[4,8,6016]{2,1,0:T(8,128)(2,1)} %broadcast_in_dim.30), calls=%async_computation.2 | async-start | bytes 770048 | tf_op jit(solution)/shard_map/all_to_all | solution.py:28
  45.8 41.6 %collective-permute-start = (bf16[1792,512]{1,0:T(8,128)(2,1)}, bf16[1792,512]{1,0:T(8,128)(2,1)}, u32[]{:S(2)}, u32[]{:S(2)}) collective-permute-start(bf16[1792,512]{1,0:T(8,128)(2,1)} %own_ref.5), channel_id=1, source_target_pairs={{0,1},{1,0},{2,3},{3,2},{4,5},{5,4},{6,7},{7,6},{8,9},{9,8},{10,11... | collective-permute-start | bytes 5505032 | tf_op jit(solution)/shard_map/ppermute | solution.py:220
  69.4 17.8 %all-to-all-start.3 = ((bf16[16,4,1792]{2,1,0:T(4,128)(2,1)}), bf16[16,4,1792]{2,1,0:T(4,128)(2,1)S(1)}, u32[]{:S(2)}, u32[]{:S(2)}) async-start(bf16[16,4,1792]{2,1,0:T(4,128)(2,1)} %bitcast.17), calls=%async_computation.3 | async-start | bytes 458752 | tf_op jit(solution)/shard_map/all_to_all | solution.py:28
  78.1 1.5 copy-start
  80.7 22.8 %collective-permute-start.1 = (bf16[512,1792]{1,0:T(8,128)(2,1)S(1)}, bf16[512,1792]{1,0:T(8,128)(2,1)}, u32[]{:S(2)}, u32[]{:S(2)}) collective-permute-start(bf16[512,1792]{1,0:T(8,128)(2,1)S(1)} %shard_map.65.own_ref), channel_id=1, source_target_pairs={{0,1},{1,0},{2,3},{3,2},{4,5},{5,4},{6,7},{7,6},{8,9},{9,8},{10,11... | collective-permute-start | bytes 5505032 | tf_op jit(solution)/shard_map/ppermute | solution.py:222
  87.4 8.0 %copy-start.2 = (f32[64,512]{1,0:T(8,128)S(1)}, f32[64,512]{1,0:T(8,128)}, u32[]{:S(2)}) copy-start(f32[64,512]{1,0:T(8,128)} %param.6) | copy-start | bytes 393220
  87.4 16.1 %copy-start.1 = (f32[512]{0:T(512)S(1)}, f32[512]{0:T(512)}, u32[]{:S(2)}) copy-start(f32[512]{0:T(512)} %param.7) | copy-start | bytes 6148
  90.5 13.0 %all-to-all-start.4 = ((bf16[8,32,512]{2,1,0:T(8,128)(2,1)}), bf16[8,32,512]{2,1,0:T(8,128)(2,1)S(1)}, u32[]{:S(2)}, u32[]{:S(2)}) async-start(bf16[8,32,512]{2,1,0:T(8,128)(2,1)} %shard_map.64), calls=%async_computation.4 | async-start | bytes 524288 | tf_op jit(solution)/shard_map/all_to_all | solution.py:28

commit v4 on v3

v4 whole, which is shorter than its diff:
```python
import jax
import jax.numpy as jnp
from jax import lax
from jax.experimental import pallas as pl
from jax.experimental.pallas import tpu as pltpu
from jax.sharding import PartitionSpec as P

D = 16384
STEPS = 3
LANES = 128

ADAPTER_SCALING = 2.0
EPSILON = 1e-05

NEAR = [[y * 16 + far * 4 + low for y in range(2) for low in range(4)] for far in range(4)]
FAR = [[y * 16 + far * 4 + low for far in range(4)] for y in range(2) for low in range(4)]
PAIRS = [
    [src * 16 + chip * 2 + core for core in range(2) for src in near]
    for near in NEAR
    for chip in range(8)
]
CORES = [[2 * chip, 2 * chip + 1] for chip in range(8)]
CHIPS = [[2 * chip + core for chip in range(8)] for core in range(2)]
SWAP = [(i, i ^ 1) for i in range(16)]


def exchange(blocks, axis, groups):
    return lax.all_to_all(blocks, axis, 0, 0, axis_index_groups=groups, tiled=True)


def share(block, axis, groups, size):
    return exchange(jnp.broadcast_to(block[None], (size,) + block.shape), axis, groups)


def total(blocks):
    return jnp.sum(blocks.astype(jnp.float32), axis=0)


def pack(values, squares, others=None):
    high = lax.reduce_precision(squares, 8, 7)
    rest = squares - high
    middle = lax.reduce_precision(rest, 8, 7)
    parts = [values, high, middle, rest - middle]
    used = 3
    if others is not None:
        parts.append(others)
        used += others.shape[1]
    parts.append(jnp.zeros((values.shape[0], LANES - used), jnp.float32))
    return jnp.concatenate(parts, axis=1).astype(jnp.bfloat16)


def unpack(both, width, ranks):
    squares = jnp.sum(both[:, width : width + 3], axis=1, keepdims=True)
    return both[:, :width], squares, both[:, width + 3 : width + 3 + ranks]


def activate(values, squares, projected, ranks_b):
    rows = values.shape[0]
    high = lax.reduce_precision(projected, 8, 7)
    both = jnp.concatenate([high, projected - high], axis=0).astype(jnp.bfloat16)
    update = dot(both, ranks_b)
    values = values + ADAPTER_SCALING * (update[:rows] + update[rows:])
    hidden = values * lax.rsqrt(squares / D + EPSILON)
    return jax.nn.silu(hidden).astype(jnp.bfloat16)


def dot(a, b):
    return jnp.dot(a, b, preferred_element_type=jnp.float32)


def params(mib=24):
    return pltpu.CompilerParams(vmem_limit_bytes=mib * 1024 * 1024)


VMEM = pl.BlockSpec(memory_space=pltpu.VMEM)
HBM = pl.BlockSpec(memory_space=pltpu.HBM)


def up_kernel(branch_ref, current_ref, gain_ref, a_ref, own_ref, other_ref, next_ref, sent_ref, held, sems):
    units = own_ref.shape[1]
    part = units // 2
    copies = []
    for i in range(2):
        source = other_ref.at[:, pl.ds(i * part, part)]
        copies.append(pltpu.make_async_copy(source, held.at[i], sems.at[i]))
        copies[-1].start()
    current = current_ref[...] + jnp.sum(branch_ref[...].astype(jnp.float32), axis=0)
    next_ref[...] = current
    scaled = (current * gain_ref[...]).astype(jnp.bfloat16)
    squares = jnp.sum(current * current, axis=1, keepdims=True)
    high = squares.astype(jnp.bfloat16).astype(jnp.float32)
    rest = squares - high
    middle = rest.astype(jnp.bfloat16).astype(jnp.float32)
    lane = lax.broadcasted_iota(jnp.int32, (current.shape[0], LANES), 1)
    tail = jnp.where(lane == 0, high, jnp.where(lane == 1, middle, rest - middle))
    tail = jnp.where(lane < 3, tail, dot(scaled, a_ref[...]))
    sent_ref[:, pl.ds(2 * units, LANES)] = tail.astype(jnp.bfloat16)
    sent_ref[:, pl.ds(0, units)] = dot(scaled, own_ref[...]).astype(jnp.bfloat16)
    for i in range(2):
        copies[i].wait()
        sent_ref[:, pl.ds(units + i * part, part)] = dot(scaled, held[i]).astype(jnp.bfloat16)


def up(branches, current, gain, columns_a, own, other):
    rows, width = current.shape
    units = own.shape[1]
    return pl.pallas_call(
        up_kernel,
        in_specs=[VMEM] * 5 + [HBM],
        out_specs=[VMEM, VMEM],
        out_shape=[
            jax.ShapeDtypeStruct(current.shape, jnp.float32),
            jax.ShapeDtypeStruct((rows, 2 * units + LANES), jnp.bfloat16),
        ],
        scratch_shapes=[
            pltpu.VMEM((2, width, units // 2), jnp.bfloat16),
            pltpu.SemaphoreType.DMA((2,)),
        ],
        compiler_params=params(),
        cost_estimate=pl.CostEstimate(
            flops=4 * rows * width * units, bytes_accessed=4 * width * units, transcendentals=0
        ),
    )(branches, current, gain, columns_a, own, other)


def down_kernel(active_ref, own_ref, other_ref, *refs):
    out_ref, held, sems = refs[-3:]
    part = own_ref.shape[0] // 2
    copies = []
    for i in range(4):
        source = (own_ref, other_ref)[i // 2].at[pl.ds((i % 2) * part, part)]
        copies.append(pltpu.make_async_copy(source, held.at[i], sems.at[i]))
        copies[-1].start()
    branch = jnp.zeros(out_ref.shape[1:], jnp.float32)
    for i in range(4):
        copies[i].wait()
        branch = branch + dot(active_ref[:, pl.ds(i * part, part)], held[i])
    out_ref[...] = jnp.broadcast_to(branch.astype(jnp.bfloat16)[None], out_ref.shape)


def down(active, own, other, copies, *after):
    rows = active.shape[0]
    units, width = own.shape
    return pl.pallas_call(
        down_kernel,
        in_specs=[VMEM, HBM, HBM] + [pl.BlockSpec(memory_space=pl.ANY)] * len(after),
        out_specs=VMEM,
        out_shape=jax.ShapeDtypeStruct((copies, rows, width), jnp.bfloat16),
        scratch_shapes=[
            pltpu.VMEM((4, units // 2, width), jnp.bfloat16),
            pltpu.SemaphoreType.DMA((4,)),
        ],
        compiler_params=params(52),
        cost_estimate=pl.CostEstimate(
            flops=4 * rows * width * units, bytes_accessed=4 * width * units, transcendentals=0
        ),
    )(active, own, other, *after)


def per_device(stream, norm_gain, frozen_up_weight, factor_a, factor_b, down_projection_matrix):
    rows, width = stream.shape
    units = frozen_up_weight.shape[1]
    half = rows // 2
    first = lax.axis_index("tp") % 2 == 0
    gain = norm_gain[None]

    up_own, down_own = frozen_up_weight, down_projection_matrix
    up_other = lax.ppermute(up_own, "tp", SWAP)
    down_other = lax.ppermute(down_own, "tp", SWAP)

    ranks_a = share(factor_a, "tp", None, 16).reshape(-1, width)
    ranks = ranks_a.shape[0]
    columns_a = jnp.pad(ranks_a.T, ((0, 0), (3, LANES - 3 - ranks)))

    scaled = (stream * gain).astype(jnp.bfloat16)
    squares = jnp.sum(stream * stream, axis=1, keepdims=True)
    projected = dot(scaled, columns_a)[:, 3 : 3 + ranks]
    sent = pack(dot(scaled, up_own), squares, projected).reshape(8, rows // 8, -1)
    end = sent.shape[2]
    quarter = units // 4
    own_b = factor_b.reshape(8, quarter)
    own_b = jnp.pad(own_b, ((0, 0), (0, -(end + quarter) % LANES)))
    sent = jnp.concatenate([sent, jnp.broadcast_to(own_b[None], (8,) + own_b.shape)], axis=2)
    near = exchange(sent, "src", NEAR)
    sent = pack(*unpack(total(near[:, :, :end]), units, ranks))
    sent = jnp.concatenate(
        [sent] + [near[i, :, end : end + quarter] for i in range(8)], axis=1
    )
    far = share(sent, "src", FAR, 4)
    own_b = far[:, :, end:].reshape(4, 8, 2, 4, quarter).transpose(2, 0, 3, 1, 4)
    own_b = own_b.reshape(ranks, units)
    active = activate(*unpack(total(far[:, :, :end]), units, ranks), own_b)
    other_b = lax.ppermute(own_b, "tp", SWAP)
    ranks_b = jnp.concatenate([own_b, other_b], axis=1)

    sent = jnp.broadcast_to(
        active.reshape(2, 1, rows // 16, units), (2, 8, rows // 16, units)
    ).reshape(16, rows // 16, units)
    active = exchange(sent, ("src", "tp"), PAIRS).reshape(2, half, units)
    active = jnp.concatenate(
        [jnp.where(first, active[0], active[1]), jnp.where(first, active[1], active[0])], axis=1
    )
    by_core = stream.reshape(8, 2, rows // 16, width)
    current = jnp.where(first, by_core[:, 0], by_core[:, 1]).reshape(half, width)
    branches = down(active, down_own, down_other, 8, up_other, ranks_b, current)
    branches = exchange(branches, "tp", CHIPS)

    for step in range(1, STEPS):
        current, sent = up(branches, current, gain, columns_a, up_own, up_other)
        near = total(exchange(sent.reshape(8, half // 8, -1), "src", NEAR))
        far = total(share(pack(*unpack(near, 2 * units, ranks)), "src", FAR, 4))
        active = activate(*unpack(far, 2 * units, ranks), ranks_b)
        active = share(active, "src", NEAR, 8).reshape(half, 2 * units)
        branches = exchange(down(active, down_own, down_other, 8), "tp", CHIPS)
    current = current + total(branches)
    by_core = share(current, "tp", CORES, 2).reshape(2, 8, rows // 16, width)
    return by_core.transpose(1, 0, 2, 3).reshape(rows, width)


def solution(mesh):
    in_specs = (
        P(None, "src"),
        P("src"),
        P("src", "tp"),
        P("tp", "src"),
        P("src", "tp"),
        P("tp", "src"),
    )
    out_specs = P(None, "src")
    return jax.shard_map(
        per_device, mesh=mesh, in_specs=in_specs, out_specs=out_specs, check_vma=False
    )
```

time: 223 us -> 220 us (0.987)
    ppermute x1, starting transfers between devices: 4.79 us -> 1.92 us  [per_device(): down_other = lax.ppermute(down_own, 'tp', SWAP)]
    ppermute x1, starting transfers between devices: 2.02 us -> 4.79 us  [per_device(): up_other = lax.ppermute(up_own, 'tp', SWAP)]
    pallas_call x6 -> x5, Pallas kernels: 12.8 us -> 11.4 us  [the longest x3 7.68 us: down(): pl.pallas_call(down_kernel, in_specs=[VMEM, HBM, HBM] + [pl.BlockSpec(mem...]
  transfers between devices with their start and end apart: 6 -> 7, of which waited for: 4 -> 5; matrix products, arithmetic and copies ran while one was open for 3% -> 3% of each run, Pallas kernels for 2% -> 0%
where the time goes in v4:
time: 220 us; the launch traced here: 219 us
  blocking collectives  118 us (54%)
  starting transfers between devices  43.8 us (20%)
  waiting for transfers between devices  32.1 us (15%)
  Pallas kernels  11.4 us (5%)
  local copies, waits for them, and re-layouts  7.59 us (3%)
  other arithmetic  2.91 us (1%)
  matrix products  2.75 us (1%)
    all_to_all x10, blocking collectives, exchange(): lax.all_to_all(blocks, axis, 0, 0, axis_index_groups=groups, tiled=True)  118 us
    all_to_all x4, starting transfers between devices, exchange(): lax.all_to_all(blocks, axis, 0, 0, axis_index_groups=groups, tiled=True)  35.1 us
    all_to_all x4, waiting for transfers between devices, exchange(): lax.all_to_all(blocks, axis, 0, 0, axis_index_groups=groups, tiled=True)  30.7 us
    pallas_call x3, Pallas kernels, down(): pl.pallas_call(down_kernel, in_specs=[VMEM, HBM, HBM] + [pl.BlockSpec(mem...  7.68 us
    ppermute x1, starting transfers between devices, per_device(): up_other = lax.ppermute(up_own, 'tp', SWAP)  4.79 us
  transfers between devices with their start and end apart: 7, of which 5 were waited for; matrix products, arithmetic and copies ran while one was open for 3% of the time, Pallas kernels for 0%

profile of v4, /device:TPU:1, one launch (start us, length us, event | category | flops | bytes accessed | tf_op | source)
XLA Modules:
  0.0 219.2 jit_solution(5714738418694792453)
XLA Ops:
  0.0 1.4 broadcast_in_dim.26
  1.4 10.2 %all-to-all-start = ((bf16[16,4,512]{2,1,0:T(4,128)(2,1)}), bf16[16,4,512]{2,1,0:T(4,128)(2,1)S(1)}, u32[]{:S(2)}, u32[]{:S(2)}) async-start(bf16[16,4,512]{2,1,0:T(4,128)(2,1)} %broadcast_in_dim.26), calls=%async_computation | async-start | bytes 131072 | tf_op jit(solution)/shard_map/all_to_all | solution.py:28
  11.6 1.0 multiply_reduce_fusion
  12.7 2.0 fusion
  14.8 0.1 copy.76
  15.0 0.1 copy.75
  15.1 0.1 copy.74
  15.2 3.8 %all-to-all-done = bf16[16,4,512]{2,1,0:T(4,128)(2,1)S(1)} async-done(((bf16[16,4,512]{2,1,0:T(4,128)(2,1)}), bf16[16,4,512]{2,1,0:T(4,128)(2,1)S(1)}, u32[]{:S(2)}, u32[]{:S(2)}) %all-to-all-start) | async-done | bytes 65568 | tf_op jit(solution)/shard_map/all_to_all | solution.py:28
  19.0 0.1 copy.73
  19.2 0.2 fusion.13
  19.6 13.0 %all_to_all.70 = bf16[8,8,2432]{2,1,0:T(8,128)(2,1)S(1)} all-to-all(bf16[8,8,2432]{2,1,0:T(8,128)(2,1)S(1)} %concatenate.55), channel_id=1, replica_groups={{0,16,32,48,256,272,288,304},{64,80,96,112,320,336,352,368},{128,144,16..., dimensions={0} | all-to-all | bytes 622592 | tf_op jit(solution)/shard_map/all_to_all | solution.py:28
  33.3 0.7 broadcast_in_dim.30
  34.1 12.1 %all-to-all-start.2 = ((bf16[4,8,5504]{2,1,0:T(8,128)(2,1)}), bf16[4,8,5504]{2,1,0:T(8,128)(2,1)S(1)}, u32[]{:S(2)}, u32[]{:S(2)}) async-start(bf16[4,8,5504]{2,1,0:T(8,128)(2,1)} %broadcast_in_dim.30), calls=%async_computation.2 | async-start | bytes 704512 | tf_op jit(solution)/shard_map/all_to_all | solution.py:28
  46.2 4.8 %collective-permute-start.1 = (bf16[512,1792]{1,0:T(8,128)(2,1)S(1)}, bf16[512,1792]{1,0:T(8,128)(2,1)}, u32[]{:S(2)}, u32[]{:S(2)}) collective-permute-start(bf16[512,1792]{1,0:T(8,128)(2,1)S(1)} %copy-done), channel_id=1, source_target_pairs={{0,1},{1,0},{2,3},{3,2},{4,5},{5,4},{6,7},{7,6},{8,9},{9,8},{10,11... | collective-permute-start | bytes 5505032 | tf_op jit(solution)/shard_map/ppermute | solution.py:168
  51.0 1.9 collective-permute-start
  52.9 13.2 %all-to-all-done.2 = bf16[4,8,5504]{2,1,0:T(8,128)(2,1)S(1)} async-done(((bf16[4,8,5504]{2,1,0:T(8,128)(2,1)}), bf16[4,8,5504]{2,1,0:T(8,128)(2,1)S(1)}, u32[]{:S(2)}, u32[]{:S(2)}) %all-to-all-start.2) | async-done | bytes 352288 | tf_op jit(solution)/shard_map/all_to_all | solution.py:28
  66.4 0.4 reshape.297
  66.8 0.3 reshape.298
  67.1 0.1 fusion.17
  67.4 0.8 broadcast_in_dim.32
  68.1 9.2 %all-to-all-start.3 = ((bf16[16,4,1792]{2,1,0:T(4,128)(2,1)}), bf16[16,4,1792]{2,1,0:T(4,128)(2,1)S(1)}, u32[]{:S(2)}, u32[]{:S(2)}) async-start(bf16[16,4,1792]{2,1,0:T(4,128)(2,1)} %bitcast.13), calls=%async_computation.3 | async-start | bytes 458752 | tf_op jit(solution)/shard_map/all_to_all | solution.py:28
  77.5 2.0 collective-permute-start.2
  79.5 1.3 collective-permute-done.2
  80.9 5.7 %all-to-all-done.3 = bf16[16,4,1792]{2,1,0:T(4,128)(2,1)S(1)} async-done(((bf16[16,4,1792]{2,1,0:T(4,128)(2,1)}), bf16[16,4,1792]{2,1,0:T(4,128)(2,1)S(1)}, u32[]{:S(2)}, u32[]{:S(2)}) %all-to-all-start.3) | async-done | bytes 229408 | tf_op jit(solution)/shard_map/all_to_all | solution.py:28
  86.8 3.0 %shard_map.64 = bf16[8,32,512]{2,1,0:T(8,128)(2,1)} custom-call(bf16[32,3584]{1,0:T(8,128)(2,1)S(1)} %pad_maximum_fusion.active_ref, bf16[1792,512]{1,0:T(8,128)(2,1)} %own_ref.9, bf16[1792,512]{1,0:T(8,128)(2,1)} %collective-permute-done.other_ref, bf16[512,1792]{1,0:T(8,128)(2,1)} %collective-permute-done.1.refs_0_.other_ref, ...), custom_call_target="tpu_custom_call" | custom-call | flops 117440512 | bytes 3670016 | tf_op jit(solution)/shard_map/pallas_call | solution.py:144
  89.9 3.5 %all-to-all-start.4 = ((bf16[8,32,512]{2,1,0:T(8,128)(2,1)}), bf16[8,32,512]{2,1,0:T(8,128)(2,1)S(1)}, u32[]{:S(2)}, u32[]{:S(2)}) async-start(bf16[8,32,512]{2,1,0:T(8,128)(2,1)} %shard_map.64), calls=%async_computation.4 | async-start | bytes 524288 | tf_op jit(solution)/shard_map/all_to_all | solution.py:28
  93.5 8.0 %all-to-all-done.4.branch_ref = bf16[8,32,512]{2,1,0:T(8,128)(2,1)S(1)} async-done(((bf16[8,32,512]{2,1,0:T(8,128)(2,1)}), bf16[8,32,512]{2,1,0:T(8,128)(2,1)S(1)}, u32[]{:S(2)}, u32[]{:S(2)}) %all-to-all-start.4) | async-done | bytes 262176 | tf_op jit(solution)/shard_map/all_to_all | solution.py:28
  101.5 1.8 shard_map.65
  103.5 9.7 %all_to_all.71 = bf16[8,4,3712]{2,1,0:T(4,128)(2,1)S(1)} all-to-all(bf16[8,4,3712]{2,1,0:T(4,128)(2,1)S(1)} %reshape.301), channel_id=1, replica_groups={{0,16,32,48,256,272,288,304},{64,80,96,112,320,336,352,368},{128,144,16..., dimensions={0} | all-to-all | bytes 475136 | tf_op jit(solution)/shard_map/all_to_all | solution.py:28
  113.3 0.1 slice_reduce_fusion.5
  114.0 14.7 %all_to_all.72 = bf16[4,4,3712]{2,1,0:T(4,128)(2,1)S(1)} all-to-all(bf16[4,4,3712]{2,1,0:T(4,128)(2,1)S(1)} %broadcast_in_dim.34), channel_id=1, replica_groups={{0,64,128,192},{16,80,144,208},{32,96,160,224},{48,112,176,240},{256,32..., dimensions={0} | all-to-all | bytes 237568 | tf_op jit(solution)/shard_map/all_to_all | solution.py:28
  128.8 0.1 slice_reduce_fusion.4
  129.0 0.2 fusion.23
  129.1 0.1 fusion.11
  129.3 10.6 %all_to_all.73 = bf16[8,4,3584]{2,1,0:T(4,128)(2,1)S(1)} all-to-all(bf16[8,4,3584]{2,1,0:T(4,128)(2,1)S(1)} %broadcast_in_dim.35), channel_id=1, replica_groups={{0,16,32,48,256,272,288,304},{64,80,96,112,320,336,352,368},{128,144,16..., dimensions={0} | all-to-all | bytes 458752 | tf_op jit(solution)/shard_map/all_to_all | solution.py:28
  139.9 2.3 %shard_map.66 = bf16[8,32,512]{2,1,0:T(8,128)(2,1)S(1)} custom-call(bf16[32,3584]{1,0:T(8,128)(2,1)S(1)} %reshape.302.active_ref, bf16[1792,512]{1,0:T(8,128)(2,1)} %own_ref.9, bf16[1792,512]{1,0:T(8,128)(2,1)} %collective-permute-done.other_ref), custom_call_target="tpu_custom_call" | custom-call | flops 117440512 | bytes 3670016 | tf_op jit(solution)/shard_map/pallas_call | solution.py:144
  142.3 11.2 %all_to_all.74.branch_ref = bf16[8,32,512]{2,1,0:T(8,128)(2,1)S(1)} all-to-all(bf16[8,32,512]{2,1,0:T(8,128)(2,1)S(1)} %shard_map.66), channel_id=1, replica_groups={{0,2,4,6,8,10,12,14},{1,3,5,7,9,11,13,15},{16,18,20,22,24,26,28,30},{17..., dimensions={0} | all-to-all | bytes 524288 | tf_op jit(solution)/shard_map/all_to_all | solution.py:28
  153.5 1.8 shard_map.67
  155.4 9.6 %all_to_all.75 = bf16[8,4,3712]{2,1,0:T(4,128)(2,1)S(1)} all-to-all(bf16[8,4,3712]{2,1,0:T(4,128)(2,1)S(1)} %reshape.303), channel_id=1, replica_groups={{0,16,32,48,256,272,288,304},{64,80,96,112,320,336,352,368},{128,144,16..., dimensions={0} | all-to-all | bytes 475136 | tf_op jit(solution)/shard_map/all_to_all | solution.py:28
  165.2 0.1 slice_reduce_fusion.3
  165.9 14.6 %all_to_all.76 = bf16[4,4,3712]{2,1,0:T(4,128)(2,1)S(1)} all-to-all(bf16[4,4,3712]{2,1,0:T(4,128)(2,1)S(1)} %broadcast_in_dim.36), channel_id=1, replica_groups={{0,64,128,192},{16,80,144,208},{32,96,160,224},{48,112,176,240},{256,32..., dimensions={0} | all-to-all | bytes 237568 | tf_op jit(solution)/shard_map/all_to_all | solution.py:28
  180.8 0.2 fusion.27
  180.9 0.1 fusion.12
  181.1 9.7 %all_to_all.77 = bf16[8,4,3584]{2,1,0:T(4,128)(2,1)S(1)} all-to-all(bf16[8,4,3584]{2,1,0:T(4,128)(2,1)S(1)} %broadcast_in_dim.37), channel_id=1, replica_groups={{0,16,32,48,256,272,288,304},{64,80,96,112,320,336,352,368},{128,144,16..., dimensions={0} | all-to-all | bytes 458752 | tf_op jit(solution)/shard_map/all_to_all | solution.py:28
  190.9 2.3 %shard_map.68 = bf16[8,32,512]{2,1,0:T(8,128)(2,1)S(1)} custom-call(bf16[32,3584]{1,0:T(8,128)(2,1)S(1)} %reshape.304.active_ref, bf16[1792,512]{1,0:T(8,128)(2,1)} %own_ref.9, bf16[1792,512]{1,0:T(8,128)(2,1)} %collective-permute-done.other_ref), custom_call_target="tpu_custom_call" | custom-call | flops 117440512 | bytes 3670016 | tf_op jit(solution)/shard_map/pallas_call | solution.py:144
  193.2 10.2 %all_to_all.78 = bf16[8,32,512]{2,1,0:T(8,128)(2,1)S(1)} all-to-all(bf16[8,32,512]{2,1,0:T(8,128)(2,1)S(1)} %shard_map.68), channel_id=1, replica_groups={{0,2,4,6,8,10,12,14},{1,3,5,7,9,11,13,15},{16,18,20,22,24,26,28,30},{17..., dimensions={0} | all-to-all | bytes 524288 | tf_op jit(solution)/shard_map/all_to_all | solution.py:28
  203.5 14.9 %all_to_all.79 = f32[2,32,512]{2,1,0:T(8,128)S(1)} all-to-all(f32[2,32,512]{2,1,0:T(8,128)S(1)} %broadcast_in_dim.38), channel_id=1, replica_groups={{0,1},{2,3},{4,5},{6,7},{8,9},{10,11},{12,13},{14,15},{16,17},{18,19},{..., dimensions={0} | all-to-all | bytes 262144 | tf_op jit(solution)/shard_map/all_to_all | solution.py:28
  218.5 0.7 reshape.306
  (88 shorter events, 4.2 us)
Async XLA Ops:
  0.0 19.1 %copy-start.2 = (f32[64,512]{1,0:T(8,128)S(1)}, f32[64,512]{1,0:T(8,128)}, u32[]{:S(2)}) copy-start(f32[64,512]{1,0:T(8,128)} %param.6) | copy-start | bytes 393220
  0.0 19.1 %copy-start.1 = (f32[512]{0:T(512)S(1)}, f32[512]{0:T(512)}, u32[]{:S(2)}) copy-start(f32[512]{0:T(512)} %param.7) | copy-start | bytes 6148
  0.0 14.7 %copy-start.3 = (bf16[2,1792]{1,0:T(2,128)(2,1)S(1)}, bf16[2,1792]{1,0:T(2,128)(2,1)}, u32[]{:S(2)}) copy-start(bf16[2,1792]{1,0:T(2,128)(2,1)} %param.10) | copy-start | bytes 21508
  1.4 17.6 %all-to-all-start = ((bf16[16,4,512]{2,1,0:T(4,128)(2,1)}), bf16[16,4,512]{2,1,0:T(4,128)(2,1)S(1)}, u32[]{:S(2)}, u32[]{:S(2)}) async-start(bf16[16,4,512]{2,1,0:T(4,128)(2,1)} %broadcast_in_dim.26), calls=%async_computation | async-start | bytes 131072 | tf_op jit(solution)/shard_map/all_to_all | solution.py:28
  19.2 27.0 %copy-start = (bf16[512,1792]{1,0:T(8,128)(2,1)S(1)}, bf16[512,1792]{1,0:T(8,128)(2,1)}, u32[]{:S(2)}) copy-start(bf16[512,1792]{1,0:T(8,128)(2,1)} %own_ref.8) | copy-start | bytes 5505028
  34.1 32.1 %all-to-all-start.2 = ((bf16[4,8,5504]{2,1,0:T(8,128)(2,1)}), bf16[4,8,5504]{2,1,0:T(8,128)(2,1)S(1)}, u32[]{:S(2)}, u32[]{:S(2)}) async-start(bf16[4,8,5504]{2,1,0:T(8,128)(2,1)} %broadcast_in_dim.30), calls=%async_computation.2 | async-start | bytes 704512 | tf_op jit(solution)/shard_map/all_to_all | solution.py:28
  46.2 40.6 %collective-permute-start.1 = (bf16[512,1792]{1,0:T(8,128)(2,1)S(1)}, bf16[512,1792]{1,0:T(8,128)(2,1)}, u32[]{:S(2)}, u32[]{:S(2)}) collective-permute-start(bf16[512,1792]{1,0:T(8,128)(2,1)S(1)} %copy-done), channel_id=1, source_target_pairs={{0,1},{1,0},{2,3},{3,2},{4,5},{5,4},{6,7},{7,6},{8,9},{9,8},{10,11... | collective-permute-start | bytes 5505032 | tf_op jit(solution)/shard_map/ppermute | solution.py:168
  51.0 35.8 %collective-permute-start = (bf16[1792,512]{1,0:T(8,128)(2,1)}, bf16[1792,512]{1,0:T(8,128)(2,1)}, u32[]{:S(2)}, u32[]{:S(2)}) collective-permute-start(bf16[1792,512]{1,0:T(8,128)(2,1)} %own_ref.9), channel_id=1, source_target_pairs={{0,1},{1,0},{2,3},{3,2},{4,5},{5,4},{6,7},{7,6},{8,9},{9,8},{10,11... | collective-permute-start | bytes 5505032 | tf_op jit(solution)/shard_map/ppermute | solution.py:169
  68.1 18.5 %all-to-all-start.3 = ((bf16[16,4,1792]{2,1,0:T(4,128)(2,1)}), bf16[16,4,1792]{2,1,0:T(4,128)(2,1)S(1)}, u32[]{:S(2)}, u32[]{:S(2)}) async-start(bf16[16,4,1792]{2,1,0:T(4,128)(2,1)} %bitcast.13), calls=%async_computation.3 | async-start | bytes 458752 | tf_op jit(solution)/shard_map/all_to_all | solution.py:28
  77.5 3.4 %collective-permute-start.2 = (bf16[64,1792]{1,0:T(8,128)(2,1)S(1)}, bf16[64,1792]{1,0:T(8,128)(2,1)S(1)}, u32[]{:S(2)}, u32[]{:S(2)}) collective-permute-start(bf16[64,1792]{1,0:T(8,128)(2,1)S(1)} %reshape.298), channel_id=1, source_target_pairs={{0,1},{1,0},{2,3},{3,2},{4,5},{5,4},{6,7},{7,6},{8,9},{9,8},{10,11... | collective-permute-start | bytes 688136 | tf_op jit(solution)/shard_map/ppermute | solution.py:193
  89.9 11.7 %all-to-all-start.4 = ((bf16[8,32,512]{2,1,0:T(8,128)(2,1)}), bf16[8,32,512]{2,1,0:T(8,128)(2,1)S(1)}, u32[]{:S(2)}, u32[]{:S(2)}) async-start(bf16[8,32,512]{2,1,0:T(8,128)(2,1)} %shard_map.64), calls=%async_computation.4 | async-start | bytes 524288 | tf_op jit(solution)/shard_map/all_to_all | solution.py:28

commit v5 on v4

--- a/solution.py
+++ b/solution.py
@@ -19,7 +19,6 @@
     for near in NEAR
     for chip in range(8)
 ]
-CORES = [[2 * chip, 2 * chip + 1] for chip in range(8)]
 CHIPS = [[2 * chip + core for chip in range(8)] for core in range(2)]
 SWAP = [(i, i ^ 1) for i in range(16)]
 
@@ -77,11 +76,11 @@
 
 
 def up_kernel(branch_ref, current_ref, gain_ref, a_ref, own_ref, other_ref, next_ref, sent_ref, held, sems):
-    units = own_ref.shape[1]
-    part = units // 2
+    width, units = own_ref.shape
+    part = width // 2
     copies = []
     for i in range(2):
-        source = other_ref.at[:, pl.ds(i * part, part)]
+        source = other_ref.at[pl.ds(i * part, part)]
         copies.append(pltpu.make_async_copy(source, held.at[i], sems.at[i]))
         copies[-1].start()
     current = current_ref[...] + jnp.sum(branch_ref[...].astype(jnp.float32), axis=0)
@@ -96,9 +95,11 @@
     tail = jnp.where(lane < 3, tail, dot(scaled, a_ref[...]))
     sent_ref[:, pl.ds(2 * units, LANES)] = tail.astype(jnp.bfloat16)
     sent_ref[:, pl.ds(0, units)] = dot(scaled, own_ref[...]).astype(jnp.bfloat16)
+    values = jnp.zeros((current.shape[0], units), jnp.float32)
     for i in range(2):
         copies[i].wait()
-        sent_ref[:, pl.ds(units + i * part, part)] = dot(scaled, held[i]).astype(jnp.bfloat16)
+        values = values + dot(scaled[:, i * part : (i + 1) * part], held[i])
+    sent_ref[:, pl.ds(units, units)] = values.astype(jnp.bfloat16)
 
 
 def up(branches, current, gain, columns_a, own, other):
@@ -113,7 +114,7 @@
             jax.ShapeDtypeStruct((rows, 2 * units + LANES), jnp.bfloat16),
         ],
         scratch_shapes=[
-            pltpu.VMEM((2, width, units // 2), jnp.bfloat16),
+            pltpu.VMEM((2, width // 2, units), jnp.bfloat16),
             pltpu.SemaphoreType.DMA((2,)),
         ],
         compiler_params=params(),
@@ -213,8 +214,10 @@
         active = share(active, "src", NEAR, 8).reshape(half, 2 * units)
         branches = exchange(down(active, down_own, down_other, 8), "tp", CHIPS)
     current = current + total(branches)
-    by_core = share(current, "tp", CORES, 2).reshape(2, 8, rows // 16, width)
-    return by_core.transpose(1, 0, 2, 3).reshape(rows, width)
+    own = current.reshape(8, rows // 16, width)
+    other = lax.ppermute(current, "tp", SWAP).reshape(8, rows // 16, width)
+    by_core = [jnp.where(first, own, other), jnp.where(first, other, own)]
+    return jnp.stack(by_core, axis=1).reshape(rows, width)
 
 
 def solution(mesh):

time: 220 us -> 220 us (level)
  blocking collectives: 118 us -> 103 us
  starting transfers between devices: 43.8 us -> 57.1 us
    all_to_all x10 -> x9, blocking collectives: 118 us -> 103 us  [exchange(): lax.all_to_all(blocks, axis, 0, 0, axis_index_groups=groups, tiled=True)]
    ppermute x0 -> x1, starting transfers between devices: none -> 13.3 us  [per_device(): other = lax.ppermute(current, 'tp', SWAP).reshape(8, rows // 16, width)]
  transfers between devices with their start and end apart: 7 -> 8, of which waited for: 5 -> 6; matrix products, arithmetic and copies ran while one was open for 3% -> 3% of each run, Pallas kernels for 0% -> 0%
where the time goes in v5:
time: 220 us; the launch traced here: 219 us
  blocking collectives  103 us (47%)
  starting transfers between devices  57.1 us (26%)
  waiting for transfers between devices  32.9 us (15%)
  Pallas kernels  11.6 us (5%)
  local copies, waits for them, and re-layouts  7.49 us (3%)
  other arithmetic  2.96 us (1%)
  matrix products  2.75 us (1%)
    all_to_all x9, blocking collectives, exchange(): lax.all_to_all(blocks, axis, 0, 0, axis_index_groups=groups, tiled=True)  103 us
    all_to_all x4, starting transfers between devices, exchange(): lax.all_to_all(blocks, axis, 0, 0, axis_index_groups=groups, tiled=True)  35.1 us
    all_to_all x4, waiting for transfers between devices, exchange(): lax.all_to_all(blocks, axis, 0, 0, axis_index_groups=groups, tiled=True)  30.7 us
    ppermute x1, starting transfers between devices, per_device(): other = lax.ppermute(current, 'tp', SWAP).reshape(8, rows // 16, width)  13.3 us
    pallas_call x3, Pallas kernels, down(): pl.pallas_call(down_kernel, in_specs=[VMEM, HBM, HBM] + [pl.BlockSpec(mem...  7.68 us
    ppermute x1, starting transfers between devices, per_device(): up_other = lax.ppermute(up_own, 'tp', SWAP)  4.79 us
  transfers between devices with their start and end apart: 8, of which 6 were waited for; matrix products, arithmetic and copies ran while one was open for 3% of the time, Pallas kernels for 0%

profile of v5, /device:TPU:1, one launch (start us, length us, event | category | flops | bytes accessed | tf_op | source)
XLA Modules:
  0.0 218.7 jit_solution(17145925850304569575)
XLA Ops:
  0.0 1.4 broadcast_in_dim.24
  1.4 10.2 %all-to-all-start = ((bf16[16,4,512]{2,1,0:T(4,128)(2,1)}), bf16[16,4,512]{2,1,0:T(4,128)(2,1)S(1)}, u32[]{:S(2)}, u32[]{:S(2)}) async-start(bf16[16,4,512]{2,1,0:T(4,128)(2,1)} %broadcast_in_dim.24), calls=%async_computation | async-start | bytes 131072 | tf_op jit(solution)/shard_map/all_to_all | solution.py:27
  11.6 1.0 multiply_reduce_fusion
  12.7 2.0 fusion
  14.8 0.1 copy.43
  15.0 0.1 copy.42
  15.1 0.1 copy.41
  15.2 3.8 %all-to-all-done = bf16[16,4,512]{2,1,0:T(4,128)(2,1)S(1)} async-done(((bf16[16,4,512]{2,1,0:T(4,128)(2,1)}), bf16[16,4,512]{2,1,0:T(4,128)(2,1)S(1)}, u32[]{:S(2)}, u32[]{:S(2)}) %all-to-all-start) | async-done | bytes 65568 | tf_op jit(solution)/shard_map/all_to_all | solution.py:27
  19.0 0.1 copy.40
  19.2 0.2 fusion.13
  19.6 13.0 %all_to_all.65 = bf16[8,8,2432]{2,1,0:T(8,128)(2,1)S(1)} all-to-all(bf16[8,8,2432]{2,1,0:T(8,128)(2,1)S(1)} %concatenate.55), channel_id=1, replica_groups={{0,16,32,48,256,272,288,304},{64,80,96,112,320,336,352,368},{128,144,16..., dimensions={0} | all-to-all | bytes 622592 | tf_op jit(solution)/shard_map/all_to_all | solution.py:27
  33.3 0.7 broadcast_in_dim.28
  34.1 12.1 %all-to-all-start.2 = ((bf16[4,8,5504]{2,1,0:T(8,128)(2,1)}), bf16[4,8,5504]{2,1,0:T(8,128)(2,1)S(1)}, u32[]{:S(2)}, u32[]{:S(2)}) async-start(bf16[4,8,5504]{2,1,0:T(8,128)(2,1)} %broadcast_in_dim.28), calls=%async_computation.2 | async-start | bytes 704512 | tf_op jit(solution)/shard_map/all_to_all | solution.py:27
  46.2 4.8 %collective-permute-start.1 = (bf16[512,1792]{1,0:T(8,128)(2,1)S(1)}, bf16[512,1792]{1,0:T(8,128)(2,1)}, u32[]{:S(2)}, u32[]{:S(2)}) collective-permute-start(bf16[512,1792]{1,0:T(8,128)(2,1)S(1)} %copy-done), channel_id=1, source_target_pairs={{0,1},{1,0},{2,3},{3,2},{4,5},{5,4},{6,7},{7,6},{8,9},{9,8},{10,11... | collective-permute-start | bytes 5505032 | tf_op jit(solution)/shard_map/ppermute | solution.py:169
  51.0 1.9 collective-permute-start
  52.9 13.2 %all-to-all-done.2 = bf16[4,8,5504]{2,1,0:T(8,128)(2,1)S(1)} async-done(((bf16[4,8,5504]{2,1,0:T(8,128)(2,1)}), bf16[4,8,5504]{2,1,0:T(8,128)(2,1)S(1)}, u32[]{:S(2)}, u32[]{:S(2)}) %all-to-all-start.2) | async-done | bytes 352288 | tf_op jit(solution)/shard_map/all_to_all | solution.py:27
  66.4 0.4 reshape.333
  66.8 0.3 reshape.334
  67.1 0.1 fusion.17
  67.4 0.8 broadcast_in_dim.30
  68.1 9.2 %all-to-all-start.3 = ((bf16[16,4,1792]{2,1,0:T(4,128)(2,1)}), bf16[16,4,1792]{2,1,0:T(4,128)(2,1)S(1)}, u32[]{:S(2)}, u32[]{:S(2)}) async-start(bf16[16,4,1792]{2,1,0:T(4,128)(2,1)} %bitcast.13), calls=%async_computation.3 | async-start | bytes 458752 | tf_op jit(solution)/shard_map/all_to_all | solution.py:27
  77.5 2.0 collective-permute-start.2
  79.5 1.3 collective-permute-done.2
  80.9 5.7 %all-to-all-done.3 = bf16[16,4,1792]{2,1,0:T(4,128)(2,1)S(1)} async-done(((bf16[16,4,1792]{2,1,0:T(4,128)(2,1)}), bf16[16,4,1792]{2,1,0:T(4,128)(2,1)S(1)}, u32[]{:S(2)}, u32[]{:S(2)}) %all-to-all-start.3) | async-done | bytes 229408 | tf_op jit(solution)/shard_map/all_to_all | solution.py:27
  86.8 3.0 %shard_map.64 = bf16[8,32,512]{2,1,0:T(8,128)(2,1)} custom-call(bf16[32,3584]{1,0:T(8,128)(2,1)S(1)} %pad_maximum_fusion.active_ref, bf16[1792,512]{1,0:T(8,128)(2,1)} %own_ref.9, bf16[1792,512]{1,0:T(8,128)(2,1)} %collective-permute-done.other_ref, bf16[512,1792]{1,0:T(8,128)(2,1)} %collective-permute-done.1.refs_0_.other_ref, ...), custom_call_target="tpu_custom_call" | custom-call | flops 117440512 | bytes 3670016 | tf_op jit(solution)/shard_map/pallas_call | solution.py:145
  89.9 3.5 %all-to-all-start.4 = ((bf16[8,32,512]{2,1,0:T(8,128)(2,1)}), bf16[8,32,512]{2,1,0:T(8,128)(2,1)S(1)}, u32[]{:S(2)}, u32[]{:S(2)}) async-start(bf16[8,32,512]{2,1,0:T(8,128)(2,1)} %shard_map.64), calls=%async_computation.4 | async-start | bytes 524288 | tf_op jit(solution)/shard_map/all_to_all | solution.py:27
  93.5 8.0 %all-to-all-done.4.branch_ref = bf16[8,32,512]{2,1,0:T(8,128)(2,1)S(1)} async-done(((bf16[8,32,512]{2,1,0:T(8,128)(2,1)}), bf16[8,32,512]{2,1,0:T(8,128)(2,1)S(1)}, u32[]{:S(2)}, u32[]{:S(2)}) %all-to-all-start.4) | async-done | bytes 262176 | tf_op jit(solution)/shard_map/all_to_all | solution.py:27
  101.5 1.9 shard_map.65
  103.5 9.7 %all_to_all.66 = bf16[8,4,3712]{2,1,0:T(4,128)(2,1)S(1)} all-to-all(bf16[8,4,3712]{2,1,0:T(4,128)(2,1)S(1)} %reshape.337), channel_id=1, replica_groups={{0,16,32,48,256,272,288,304},{64,80,96,112,320,336,352,368},{128,144,16..., dimensions={0} | all-to-all | bytes 475136 | tf_op jit(solution)/shard_map/all_to_all | solution.py:27
  113.4 0.1 slice_reduce_fusion.5
  114.1 14.7 %all_to_all.67 = bf16[4,4,3712]{2,1,0:T(4,128)(2,1)S(1)} all-to-all(bf16[4,4,3712]{2,1,0:T(4,128)(2,1)S(1)} %broadcast_in_dim.32), channel_id=1, replica_groups={{0,64,128,192},{16,80,144,208},{32,96,160,224},{48,112,176,240},{256,32..., dimensions={0} | all-to-all | bytes 237568 | tf_op jit(solution)/shard_map/all_to_all | solution.py:27
  128.8 0.1 slice_reduce_fusion.4
  129.0 0.2 fusion.23
  129.2 0.1 fusion.11
  129.4 10.6 %all_to_all.68 = bf16[8,4,3584]{2,1,0:T(4,128)(2,1)S(1)} all-to-all(bf16[8,4,3584]{2,1,0:T(4,128)(2,1)S(1)} %broadcast_in_dim.33), channel_id=1, replica_groups={{0,16,32,48,256,272,288,304},{64,80,96,112,320,336,352,368},{128,144,16..., dimensions={0} | all-to-all | bytes 458752 | tf_op jit(solution)/shard_map/all_to_all | solution.py:27
  140.0 2.3 %shard_map.66 = bf16[8,32,512]{2,1,0:T(8,128)(2,1)S(1)} custom-call(bf16[32,3584]{1,0:T(8,128)(2,1)S(1)} %reshape.338.active_ref, bf16[1792,512]{1,0:T(8,128)(2,1)} %own_ref.9, bf16[1792,512]{1,0:T(8,128)(2,1)} %collective-permute-done.other_ref), custom_call_target="tpu_custom_call" | custom-call | flops 117440512 | bytes 3670016 | tf_op jit(solution)/shard_map/pallas_call | solution.py:145
  142.4 11.2 %all_to_all.69.branch_ref = bf16[8,32,512]{2,1,0:T(8,128)(2,1)S(1)} all-to-all(bf16[8,32,512]{2,1,0:T(8,128)(2,1)S(1)} %shard_map.66), channel_id=1, replica_groups={{0,2,4,6,8,10,12,14},{1,3,5,7,9,11,13,15},{16,18,20,22,24,26,28,30},{17..., dimensions={0} | all-to-all | bytes 524288 | tf_op jit(solution)/shard_map/all_to_all | solution.py:27
  153.6 1.9 shard_map.67
  155.6 9.6 %all_to_all.70 = bf16[8,4,3712]{2,1,0:T(4,128)(2,1)S(1)} all-to-all(bf16[8,4,3712]{2,1,0:T(4,128)(2,1)S(1)} %reshape.339), channel_id=1, replica_groups={{0,16,32,48,256,272,288,304},{64,80,96,112,320,336,352,368},{128,144,16..., dimensions={0} | all-to-all | bytes 475136 | tf_op jit(solution)/shard_map/all_to_all | solution.py:27
  166.1 14.6 %all_to_all.71 = bf16[4,4,3712]{2,1,0:T(4,128)(2,1)S(1)} all-to-all(bf16[4,4,3712]{2,1,0:T(4,128)(2,1)S(1)} %broadcast_in_dim.34), channel_id=1, replica_groups={{0,64,128,192},{16,80,144,208},{32,96,160,224},{48,112,176,240},{256,32..., dimensions={0} | all-to-all | bytes 237568 | tf_op jit(solution)/shard_map/all_to_all | solution.py:27
  180.7 0.1 slice_reduce_fusion.2
  180.9 0.2 fusion.27
  181.3 9.7 %all_to_all.72 = bf16[8,4,3584]{2,1,0:T(4,128)(2,1)S(1)} all-to-all(bf16[8,4,3584]{2,1,0:T(4,128)(2,1)S(1)} %broadcast_in_dim.35), channel_id=1, replica_groups={{0,16,32,48,256,272,288,304},{64,80,96,112,320,336,352,368},{128,144,16..., dimensions={0} | all-to-all | bytes 458752 | tf_op jit(solution)/shard_map/all_to_all | solution.py:27
  191.0 2.3 %shard_map.68 = bf16[8,32,512]{2,1,0:T(8,128)(2,1)S(1)} custom-call(bf16[32,3584]{1,0:T(8,128)(2,1)S(1)} %reshape.340.active_ref, bf16[1792,512]{1,0:T(8,128)(2,1)} %own_ref.9, bf16[1792,512]{1,0:T(8,128)(2,1)} %collective-permute-done.other_ref), custom_call_target="tpu_custom_call" | custom-call | flops 117440512 | bytes 3670016 | tf_op jit(solution)/shard_map/pallas_call | solution.py:145
  193.4 10.2 %all_to_all.73 = bf16[8,32,512]{2,1,0:T(8,128)(2,1)S(1)} all-to-all(bf16[8,32,512]{2,1,0:T(8,128)(2,1)S(1)} %shard_map.68), channel_id=1, replica_groups={{0,2,4,6,8,10,12,14},{1,3,5,7,9,11,13,15},{16,18,20,22,24,26,28,30},{17..., dimensions={0} | all-to-all | bytes 524288 | tf_op jit(solution)/shard_map/all_to_all | solution.py:27
  203.6 13.3 %collective-permute-start.3 = (f32[32,512]{1,0:T(8,128)S(1)}, f32[32,512]{1,0:T(8,128)S(1)}, u32[]{:S(2)}, u32[]{:S(2)}) collective-permute-start(f32[32,512]{1,0:T(8,128)S(1)} %add.77), channel_id=1, source_target_pairs={{0,1},{1,0},{2,3},{3,2},{4,5},{5,4},{6,7},{7,6},{8,9},{9,8},{10,11... | collective-permute-start | bytes 196616 | tf_op jit(solution)/shard_map/ppermute | solution.py:218
  217.0 0.9 collective-permute-done.3
  218.0 0.7 reshape.341
  (91 shorter events, 4.2 us)
Async XLA Ops:
  0.0 19.1 %copy-start.2 = (f32[64,512]{1,0:T(8,128)S(1)}, f32[64,512]{1,0:T(8,128)}, u32[]{:S(2)}) copy-start(f32[64,512]{1,0:T(8,128)} %param.6) | copy-start | bytes 393220
  0.0 19.1 %copy-start.1 = (f32[512]{0:T(512)S(1)}, f32[512]{0:T(512)}, u32[]{:S(2)}) copy-start(f32[512]{0:T(512)} %param.7) | copy-start | bytes 6148
  0.0 14.7 %copy-start.3 = (bf16[2,1792]{1,0:T(2,128)(2,1)S(1)}, bf16[2,1792]{1,0:T(2,128)(2,1)}, u32[]{:S(2)}) copy-start(bf16[2,1792]{1,0:T(2,128)(2,1)} %param.10) | copy-start | bytes 21508
  1.4 17.6 %all-to-all-start = ((bf16[16,4,512]{2,1,0:T(4,128)(2,1)}), bf16[16,4,512]{2,1,0:T(4,128)(2,1)S(1)}, u32[]{:S(2)}, u32[]{:S(2)}) async-start(bf16[16,4,512]{2,1,0:T(4,128)(2,1)} %broadcast_in_dim.24), calls=%async_computation | async-start | bytes 131072 | tf_op jit(solution)/shard_map/all_to_all | solution.py:27
  19.2 27.0 %copy-start = (bf16[512,1792]{1,0:T(8,128)(2,1)S(1)}, bf16[512,1792]{1,0:T(8,128)(2,1)}, u32[]{:S(2)}) copy-start(bf16[512,1792]{1,0:T(8,128)(2,1)} %own_ref.8) | copy-start | bytes 5505028
  34.1 32.1 %all-to-all-start.2 = ((bf16[4,8,5504]{2,1,0:T(8,128)(2,1)}), bf16[4,8,5504]{2,1,0:T(8,128)(2,1)S(1)}, u32[]{:S(2)}, u32[]{:S(2)}) async-start(bf16[4,8,5504]{2,1,0:T(8,128)(2,1)} %broadcast_in_dim.28), calls=%async_computation.2 | async-start | bytes 704512 | tf_op jit(solution)/shard_map/all_to_all | solution.py:27
  46.2 40.6 %collective-permute-start.1 = (bf16[512,1792]{1,0:T(8,128)(2,1)S(1)}, bf16[512,1792]{1,0:T(8,128)(2,1)}, u32[]{:S(2)}, u32[]{:S(2)}) collective-permute-start(bf16[512,1792]{1,0:T(8,128)(2,1)S(1)} %copy-done), channel_id=1, source_target_pairs={{0,1},{1,0},{2,3},{3,2},{4,5},{5,4},{6,7},{7,6},{8,9},{9,8},{10,11... | collective-permute-start | bytes 5505032 | tf_op jit(solution)/shard_map/ppermute | solution.py:169
  51.0 35.8 %collective-permute-start = (bf16[1792,512]{1,0:T(8,128)(2,1)}, bf16[1792,512]{1,0:T(8,128)(2,1)}, u32[]{:S(2)}, u32[]{:S(2)}) collective-permute-start(bf16[1792,512]{1,0:T(8,128)(2,1)} %own_ref.9), channel_id=1, source_target_pairs={{0,1},{1,0},{2,3},{3,2},{4,5},{5,4},{6,7},{7,6},{8,9},{9,8},{10,11... | collective-permute-start | bytes 5505032 | tf_op jit(solution)/shard_map/ppermute | solution.py:170
  68.1 18.5 %all-to-all-start.3 = ((bf16[16,4,1792]{2,1,0:T(4,128)(2,1)}), bf16[16,4,1792]{2,1,0:T(4,128)(2,1)S(1)}, u32[]{:S(2)}, u32[]{:S(2)}) async-start(bf16[16,4,1792]{2,1,0:T(4,128)(2,1)} %bitcast.13), calls=%async_computation.3 | async-start | bytes 458752 | tf_op jit(solution)/shard_map/all_to_all | solution.py:27
  77.5 3.4 %collective-permute-start.2 = (bf16[64,1792]{1,0:T(8,128)(2,1)S(1)}, bf16[64,1792]{1,0:T(8,128)(2,1)S(1)}, u32[]{:S(2)}, u32[]{:S(2)}) collective-permute-start(bf16[64,1792]{1,0:T(8,128)(2,1)S(1)} %reshape.334), channel_id=1, source_target_pairs={{0,1},{1,0},{2,3},{3,2},{4,5},{5,4},{6,7},{7,6},{8,9},{9,8},{10,11... | collective-permute-start | bytes 688136 | tf_op jit(solution)/shard_map/ppermute | solution.py:194
  89.9 11.7 %all-to-all-start.4 = ((bf16[8,32,512]{2,1,0:T(8,128)(2,1)}), bf16[8,32,512]{2,1,0:T(8,128)(2,1)S(1)}, u32[]{:S(2)}, u32[]{:S(2)}) async-start(bf16[8,32,512]{2,1,0:T(8,128)(2,1)} %shard_map.64), calls=%async_computation.4 | async-start | bytes 524288 | tf_op jit(solution)/shard_map/all_to_all | solution.py:27
  203.6 14.2 %collective-permute-start.3 = (f32[32,512]{1,0:T(8,128)S(1)}, f32[32,512]{1,0:T(8,128)S(1)}, u32[]{:S(2)}, u32[]{:S(2)}) collective-permute-start(f32[32,512]{1,0:T(8,128)S(1)} %add.77), channel_id=1, source_target_pairs={{0,1},{1,0},{2,3},{3,2},{4,5},{5,4},{6,7},{7,6},{8,9},{9,8},{10,11... | collective-permute-start | bytes 196616 | tf_op jit(solution)/shard_map/ppermute | solution.py:218
